TPU v7x, 128 devices: a whole 4x4x4 slice. The times are simulated.
128 devices in a mesh: wide: 16 (over z_hi, y, core), narrow: 8 (over z_lo, x).
Axes of the slice: x: 4, y: 4, z: 4 (z_hi: 2, z_lo: 2; z = z_hi * 2 + z_lo), core: 2. Of those that a mesh axis runs over, the one named last changes fastest.
Arguments:
- weights_in: float32 [16, 64, 64, 2, 8, 128], P('wide', 'narrow'), may hold values from -6 to 6
- medium_speed: float32 [8, 8], replicated, may hold values from 0.5 to 2
- target_order: int32 [64], replicated, may hold values from 0 to 63, each once
Outputs:
- weights_out: float32 [16, 64, 64, 2, 8, 128], P('wide', 'narrow')
Inputs may be any that keep to these rules, and one draw needn't show every extreme that they name: `target_order`: a permutation of the 64 starting target boxes.
All inputs are finite; a program needn't handle non-finite values.
Results may differ from a plain program's by a relative error of at most 0.0003.
Values sent between devices are 32-bit elements; how exact they have to be, the bound alone decides.
No kernel may reach another device: no remote copies, remote signals or barrier semaphores. Data moves between devices by JAX's collectives and lax.ppermute only.
A program may use at most 128 MiB of HBM per device.

v0:
```python
import jax
import jax.numpy as jnp
from jax import lax
from jax.sharding import PartitionSpec as P

TX = 8
TY = 8
SYH = 4


level_bits = (3, 2, 1, 0)
merges_across = (1, 1, 2, 2)
merges_down = (0, 1, 1, 2)


def swapped(value, axis, stride):
    mask = 2**stride
    pairs = [(source, source ^ mask) for source in range(lax.axis_size(axis))]
    return lax.ppermute(value, axis, pairs)


def cheb_nodes():
    counter = jnp.arange(8, dtype=jnp.float32)
    return 0.5 - 0.5 * jnp.cos(jnp.pi * (2.0 * counter + 1.0) / 16.0)


def lagrange_matrix(child_bit):
    node_set = cheb_nodes()
    points = (child_bit.astype(jnp.float32) + node_set) / 2.0
    differ = points[None, :, None] - node_set[None, None, :]
    spacing = node_set[:, None] - node_set[None, :]
    diagonal = jnp.eye(8, dtype=bool)
    factors = jnp.where(
        diagonal[:, None, :], 1.0, differ / jnp.where(diagonal, 1.0, spacing)[:, None, :]
    )
    return jnp.prod(factors, axis=2)


def take_bit(number, position):
    return number >> position & 1


def phase_angles(
    step_index, box_code, target_bit, source_super, target_box, speed_rows, layout, child_bit
):
    across_boxes, down_boxes, tiles_across, tiles_down, supers_down = layout
    own_bit = level_bits[step_index]
    shift_across = merges_across[step_index]
    shift_down = merges_down[step_index]
    chosen = box_code & 15 - (1 << own_bit) | target_bit << own_bit
    whole_across = (
        4 * (source_super // supers_down) + 2 * take_bit(box_code, 1) + take_bit(box_code, 3)
    )
    whole_down = (
        4 * (source_super % supers_down) + 2 * take_bit(box_code, 0) + take_bit(box_code, 2)
    )
    side_across = 2**shift_across / across_boxes
    side_down = 2**shift_down / down_boxes
    corner_across = (whole_across >> shift_across).astype(jnp.float32) * side_across
    corner_down = (whole_down >> shift_down).astype(jnp.float32) * side_down
    tile_across = target_box // tiles_down * 2**shift_across + (
        2 * take_bit(chosen, 3) + take_bit(chosen, 1) >> 2 - shift_across
    )
    tile_down = target_box % tiles_down * 2**shift_down + (
        2 * take_bit(chosen, 2) + take_bit(chosen, 0) >> 2 - shift_down
    )
    center_across = (tile_across.astype(jnp.float32) + 0.5) / (tiles_across * 2**shift_across)
    center_down = (tile_down.astype(jnp.float32) + 0.5) / (tiles_down * 2**shift_down)
    node_set = cheb_nodes()
    along_first = node_set
    along_second = node_set
    if child_bit is not None:
        halved = (child_bit.astype(jnp.float32) + node_set) / 2.0
        if step_index % 2 == 0:
            along_first = halved
        else:
            along_second = halved
    key_across = corner_across[..., None, None] + side_across * along_first[:, None]
    key_down = corner_down[..., None, None] + side_down * along_second[None, :]
    base_across = (corner_across + 0.5 * side_across)[..., None, None]
    base_down = (corner_down + 0.5 * side_down)[..., None, None]
    key_square = key_across * key_across + key_down * key_down
    base_square = base_across * base_across + base_down * base_down
    radial = (key_square - base_square) / (jnp.sqrt(key_square) + jnp.sqrt(base_square))
    wave_scale = jnp.pi * across_boxes / 2.0
    return wave_scale * (
        center_across[..., None, None] * (key_across - base_across)
        + center_down[..., None, None] * (key_down - base_down)
        + speed_rows[..., None, None] * radial
    )


def pull_child(weights, angles, step_index, child_bit):
    shaped = weights.reshape(weights.shape[:-3] + (2, 8, 8, 16))
    real_part = shaped[..., 0, :, :, :]
    imag_part = shaped[..., 1, :, :, :]
    cosine = jnp.cos(angles)[..., None]
    sine_part = jnp.sin(angles)[..., None]
    turned_real = real_part * cosine + imag_part * sine_part
    turned_imag = imag_part * cosine - real_part * sine_part
    stacked = jnp.stack([turned_real, turned_imag], axis=-4)
    matrix = lagrange_matrix(child_bit)
    if step_index % 2 == 0:
        moved = jnp.einsum("ab,...bcd->...acd", matrix, stacked, precision=lax.Precision.HIGHEST)
    else:
        moved = jnp.einsum("ab,...cbd->...cad", matrix, stacked, precision=lax.Precision.HIGHEST)
    return moved.reshape(weights.shape)


def push_parent(summed, angles):
    shaped = summed.reshape(summed.shape[:-3] + (2, 8, 8, 16))
    real_part = shaped[..., 0, :, :, :]
    imag_part = shaped[..., 1, :, :, :]
    cosine = jnp.cos(angles)[..., None]
    sine_part = jnp.sin(angles)[..., None]
    out_real = real_part * cosine - imag_part * sine_part
    out_imag = real_part * sine_part + imag_part * cosine
    return jnp.stack([out_real, out_imag], axis=-4).reshape(summed.shape)


def merge_partner(
    weights,
    step_index,
    box_code,
    code_base,
    source_super,
    target_box,
    speed_rows,
    layout,
    device_bit,
):
    own_bit = level_bits[step_index]
    child_bit = take_bit(code_base, own_bit)
    other_bit = 1 - child_bit
    outgoing = pull_child(
        weights,
        phase_angles(
            step_index, box_code, other_bit, source_super, target_box, speed_rows, layout, child_bit
        ),
        step_index,
        child_bit,
    )
    arrived = swapped(outgoing, "wide", device_bit)
    retained = pull_child(
        weights,
        phase_angles(
            step_index, box_code, child_bit, source_super, target_box, speed_rows, layout, child_bit
        ),
        step_index,
        child_bit,
    )
    parent_angles = phase_angles(
        step_index, box_code, child_bit, source_super, target_box, speed_rows, layout, None
    )
    return push_parent(retained + arrived, parent_angles)


def local(weights_in, medium_speed, target_order):
    narrow_count = lax.axis_size("narrow")
    layout = (8 * narrow_count, 4 * SYH, TX, TY, SYH)
    local_codes = weights_in.shape[0]
    per_super = weights_in.shape[1]
    tile_count = weights_in.shape[2]
    local_bits = local_codes.bit_length() - 1
    wide_place = lax.axis_index("wide")
    narrow_place = lax.axis_index("narrow")
    code_base = wide_place * local_codes
    speed_flat = medium_speed.reshape(-1)
    weights = weights_in
    source_super = (narrow_place * per_super + jnp.arange(per_super, dtype=jnp.int32))[:, None]
    target_box = jnp.arange(tile_count, dtype=jnp.int32)
    box_code = (code_base + jnp.arange(local_codes, dtype=jnp.int32))[:, None, None]
    for step_index in range(4):
        own_bit = level_bits[step_index]
        weights = merge_partner(
            weights,
            step_index,
            box_code,
            code_base,
            source_super,
            target_box,
            speed_flat,
            layout,
            own_bit - local_bits,
        )
    ordered = jnp.swapaxes(jnp.take(weights, target_order, axis=2), 1, 2)
    return lax.all_to_all(ordered, "narrow", split_axis=1, concat_axis=2, tiled=True)


def solution(mesh):
    in_specs = (P("wide", "narrow", None, None, None, None), P(), P())
    out_specs = P("wide", "narrow", None, None, None, None)
    return jax.shard_map(local, mesh=mesh, in_specs=in_specs, out_specs=out_specs, check_vma=False)
```

profile of v0, /device:TPU:1, one launch (start us, length us, event | category | flops | bytes accessed | tf_op | source)
XLA Modules:
  0.0 570.5 jit_solution(3323364022498404404)
XLA Ops:
  1.5 7.0 %copy.195 = f32[1,8,64,2,8,128]{2,4,5,3,1,0:T(8,128)} copy(f32[1,8,64,2,8,128]{5,4,3,2,1,0:T(8,128)} %param.3) | data formatting | bytes 8388608 | tf_op args[0]
  23.0 9.9 %fusion.3 = f32[8,64,2,8,16,8]{1,5,4,3,2,0:T(8,128)} fusion(f32[1,8,64,1,8,8,16]{2,4,6,5,3,1,0:T(8,128)S(1)} %get-tuple-element.38, f32[1,8,64,1,8,8,16]{2,4,6,5,3,1,0:T(8,128)S(1)} %get-tuple-element.37, f32[8,8]{1,0:T(8,128)S(1)} %get-tuple-element.8), kind=kOutput, calls=%fused_computation.6 | convolution fusion | flops 101711872 | bytes 8388864 | tf_op jit(solution)/shard_map/ab,...bcd->...acd/dot_general | solution.py:104
  32.9 6.9 %copy.197 = f32[1,8,64,2,8,128]{5,4,3,2,1,0:T(8,128)} copy(f32[1,8,64,2,8,128]{2,4,5,3,1,0:T(8,128)} %bitcast.130) | data formatting | bytes 8388608 | tf_op jit(solution)/shard_map/reshape | solution.py:107
  44.2 11.6 %fusion = f32[8,64,2,8,16,8]{1,5,4,3,2,0:T(8,128)} fusion(f32[1,8,64,1,8,8,16]{2,4,6,5,3,1,0:T(8,128)} %get-tuple-element.48, f32[1,8,64,1,8,8,16]{2,4,6,5,3,1,0:T(8,128)} %get-tuple-element.49, f32[8,8]{1,0:T(8,128)S(1)} %get-tuple-element.8), kind=kOutput, calls=%fused_computation.2 | convolution fusion | flops 101711872 | bytes 8388864 | tf_op jit(solution)/shard_map/ab,...bcd->...acd/dot_general | solution.py:104
  55.9 6.9 %copy.198 = f32[1,8,64,2,8,128]{5,4,3,2,1,0:T(8,128)} copy(f32[1,8,64,2,8,128]{2,4,5,3,1,0:T(8,128)} %bitcast.128) | data formatting | bytes 8388608 | tf_op jit(solution)/shard_map/reshape | solution.py:107
  63.1 71.7 %collective-permute-done = f32[1,8,64,2,8,128]{5,4,3,2,1,0:T(8,128)} collective-permute-done((f32[1,8,64,2,8,128]{5,4,3,2,1,0:T(8,128)}, f32[1,8,64,2,8,128]{5,4,3,2,1,0:T(8,128)}, u32[]{:S(2)}, u32[]{:S(2)}) %collective-permute-start) | collective-permute-done | bytes 4194336 | tf_op jit(solution)/shard_map/ppermute | solution.py:19
  140.9 7.1 %copy.199 = f32[1,8,64,2,8,128]{2,5,4,3,1,0:T(8,128)} copy(f32[1,8,64,2,8,128]{5,4,3,2,1,0:T(8,128)} %add.2746) | data formatting | bytes 8388608 | tf_op jit(solution)/shard_map/add | solution.py:155
  162.3 8.1 %fusion.27 = f32[1,8,64,2,8,8,16]{2,5,6,4,3,1,0:T(8,128)S(1)} fusion(f32[1,8,64,1,8,8,16]{2,5,6,4,3,1,0:T(8,128)S(1)} %get-tuple-element.45, f32[1,8,64,1,8,8,16]{2,5,6,4,3,1,0:T(8,128)S(1)} %get-tuple-element.21, f32[8,8]{1,0:T(8,128)S(1)} %get-tuple-element.6), kind=kOutput, calls=%fused_computation.63 | convolution fusion | flops 101711872 | bytes 8388864 | tf_op jit(solution)/shard_map/ab,...cbd->...cad/dot_general | solution.py:106
  175.7 6.9 %copy.210 = f32[1,8,64,2,8,128]{5,4,3,2,1,0:T(8,128)} copy(f32[1,8,64,2,8,128]{2,5,4,3,1,0:T(8,128)} %bitcast.135) | data formatting | bytes 8388608 | tf_op jit(solution)/shard_map/reshape | solution.py:107
  185.8 7.1 %fusion.38 = (f32[8,64,8,8]{1,2,3,0:T(8,128)S(1)}, f32[8,64,8,8]{1,2,3,0:T(8,128)S(1)}, f32[8,64,8,8]{1,2,3,0:T(8,128)S(1)}, f32[8,64,8,8]{1,2,3,0:T(8,128)}, f3...) fusion(f32[8,8,8]{1,2,0:T(8,128)S(1)} %get-tuple-element.107, ...), kind=kLoop, calls=%fused_computation.83 | loop fusion | flops 720896 | bytes 1745152 | tf_op jit(solution)/shard_map/cos | solution.py:114
  192.9 10.3 %fusion.28 = f32[1,8,64,2,8,8,16]{2,5,6,4,3,1,0:T(8,128)S(1)} fusion(f32[1,8,64,1,8,8,16]{2,5,6,4,3,1,0:T(8,128)} %get-tuple-element.36, f32[1,8,64,1,8,8,16]{2,5,6,4,3,1,0:T(8,128)} %get-tuple-element.35, f32[8,8]{1,0:T(8,128)S(1)} %get-tuple-element.6), kind=kOutput, calls=%fused_computation.64 | convolution fusion | flops 101711872 | bytes 8388864 | tf_op jit(solution)/shard_map/ab,...cbd->...cad/dot_general | solution.py:106
  215.3 60.0 %collective-permute-done.1 = f32[1,8,64,2,8,128]{5,4,3,2,1,0:T(8,128)} collective-permute-done((f32[1,8,64,2,8,128]{5,4,3,2,1,0:T(8,128)}, f32[1,8,64,2,8,128]{5,4,3,2,1,0:T(8,128)}, u32[]{:S(2)}, u32[]{:S(2)}) %collective-permute-start.1) | collective-permute-done | bytes 4194336 | tf_op jit(solution)/shard_map/ppermute | solution.py:19
  281.3 7.0 %copy.243 = f32[1,8,64,2,8,128]{2,4,5,3,1,0:T(8,128)} copy(f32[1,8,64,2,8,128]{5,4,3,2,1,0:T(8,128)} %add.2797) | data formatting | bytes 8388608 | tf_op jit(solution)/shard_map/reshape | solution.py:111
  297.2 9.6 %fusion.15 = f32[8,64,2,8,16,8]{1,5,4,3,2,0:T(8,128)} fusion(f32[1,8,64,1,8,8,16]{2,4,6,5,3,1,0:T(8,128)S(1)} %get-tuple-element.44, f32[1,8,64,1,8,8,16]{2,4,6,5,3,1,0:T(8,128)S(1)} %get-tuple-element.16, f32[8,8]{1,0:T(8,128)S(1)} %get-tuple-element.7), kind=kOutput, calls=%fused_computation.22 | convolution fusion | flops 101711872 | bytes 8388864 | tf_op jit(solution)/shard_map/ab,...bcd->...acd/dot_general | solution.py:104
  306.8 7.0 %copy.216 = f32[1,8,64,2,8,128]{5,4,3,2,1,0:T(8,128)} copy(f32[1,8,64,2,8,128]{2,4,5,3,1,0:T(8,128)} %bitcast.131) | data formatting | bytes 8388608 | tf_op jit(solution)/shard_map/reshape | solution.py:107
  315.5 11.6 %fusion.12 = f32[8,64,2,8,16,8]{1,5,4,3,2,0:T(8,128)} fusion(f32[1,8,64,1,8,8,16]{2,4,6,5,3,1,0:T(8,128)} %get-tuple-element.34, f32[1,8,64,1,8,8,16]{2,4,6,5,3,1,0:T(8,128)} %get-tuple-element.33, f32[8,8]{1,0:T(8,128)S(1)} %get-tuple-element.7), kind=kOutput, calls=%fused_computation.18 | convolution fusion | flops 101711872 | bytes 8388864 | tf_op jit(solution)/shard_map/ab,...bcd->...acd/dot_general | solution.py:104
  327.1 6.9 %copy.217 = f32[1,8,64,2,8,128]{5,4,3,2,1,0:T(8,128)} copy(f32[1,8,64,2,8,128]{2,4,5,3,1,0:T(8,128)} %bitcast.129) | data formatting | bytes 8388608 | tf_op jit(solution)/shard_map/reshape | solution.py:107
  334.0 70.0 %collective-permute-done.2 = f32[1,8,64,2,8,128]{5,4,3,2,1,0:T(8,128)} collective-permute-done((f32[1,8,64,2,8,128]{5,4,3,2,1,0:T(8,128)}, f32[1,8,64,2,8,128]{5,4,3,2,1,0:T(8,128)}, u32[]{:S(2)}, u32[]{:S(2)}) %collective-permute-start.2) | collective-permute-done | bytes 4194336 | tf_op jit(solution)/shard_map/ppermute | solution.py:19
  410.1 7.0 %copy.218 = f32[1,8,64,2,8,128]{2,5,4,3,1,0:T(8,128)} copy(f32[1,8,64,2,8,128]{5,4,3,2,1,0:T(8,128)} %add.2848) | data formatting | bytes 8388608 | tf_op jit(solution)/shard_map/add | solution.py:155
  432.1 8.1 %fusion.25 = f32[1,8,64,2,8,8,16]{2,5,6,4,3,1,0:T(8,128)S(1)} fusion(f32[1,8,64,1,8,8,16]{2,5,6,4,3,1,0:T(8,128)S(1)} %get-tuple-element.32, f32[1,8,64,1,8,8,16]{2,5,6,4,3,1,0:T(8,128)S(1)} %get-tuple-element.31, f32[8,8]{1,0:T(8,128)S(1)} %get-tuple-element.5), kind=kOutput, calls=%fused_computation.61 | convolution fusion | flops 101711872 | bytes 8388864 | tf_op jit(solution)/shard_map/ab,...cbd->...cad/dot_general | solution.py:106
  445.5 6.9 %copy.229 = f32[1,8,64,2,8,128]{5,4,3,2,1,0:T(8,128)} copy(f32[1,8,64,2,8,128]{2,5,4,3,1,0:T(8,128)} %bitcast.137) | data formatting | bytes 8388608 | tf_op jit(solution)/shard_map/reshape | solution.py:107
  455.6 10.5 %fusion.26 = f32[1,8,64,2,8,8,16]{2,5,6,4,3,1,0:T(8,128)S(1)} fusion(f32[1,8,64,1,8,8,16]{2,5,6,4,3,1,0:T(8,128)} %get-tuple-element.41, f32[1,8,64,1,8,8,16]{2,5,6,4,3,1,0:T(8,128)} %get-tuple-element.9, f32[8,8]{1,0:T(8,128)S(1)} %get-tuple-element.5), kind=kOutput, calls=%fused_computation.62 | convolution fusion | flops 101711872 | bytes 8388864 | tf_op jit(solution)/shard_map/ab,...cbd->...cad/dot_general | solution.py:106
  478.2 11.7 %bitcast_add_fusion = f32[1,8,64,2,8,128]{2,5,4,3,1,0:T(8,128)} fusion(f32[1,8,64,2,8,128]{2,5,4,3,1,0:T(8,128)} %copy.230, f32[1,8,64,2,8,8,16]{2,6,5,4,3,1,0:T(8,128)} %copy.225), kind=kLoop, calls=%fused_computation.33 | loop fusion | flops 1048576 | bytes 12582912 | tf_op jit(solution)/shard_map/add | solution.py:155
  514.5 53.5 %all_to_all.18 = f32[1,64,8,2,8,128]{5,4,3,2,0,1:T(8,128)S(1)} all-to-all(f32[1,64,8,2,8,128]{5,4,3,2,0,1:T(8,128)S(1)} %fusion.24), channel_id=1, replica_groups=mesh['wide'=16,'narrow'=8] {'narrow'}, dimensions={1} | all-to-all | bytes 8388608 | tf_op jit(solution)/shard_map/all_to_all | solution.py:187
  (92 shorter events, 146.6 us)
Async XLA Ops:
  39.8 95.0 %collective-permute-start = (f32[1,8,64,2,8,128]{5,4,3,2,1,0:T(8,128)}, f32[1,8,64,2,8,128]{5,4,3,2,1,0:T(8,128)}, u32[]{:S(2)}, u32[]{:S(2)}) collective-permute-start(f32[1,8,64,2,8,128]{5,4,3,2,1,0:T(8,128)} %copy.197), channel_id=1, source_target_pairs={{0,64},{8,72},{16,80},{24,88},{32,96},{40,104},{48,112},{56,120},{... | collective-permute-start | bytes 12582920 | tf_op jit(solution)/shard_map/ppermute | solution.py:19
  175.7 10.1 %copy-start.2 = (f32[8,64,8]{1,2,0:T(8,128)S(1)}, f32[8,64,8]{1,2,0:T(8,128)}, u32[]{:S(2)}) copy-start(f32[8,64,8]{1,2,0:T(8,128)} %get-tuple-element.167) | copy-start | bytes 49156
  175.7 10.1 %copy-start.3 = (f32[8,64,8]{1,2,0:T(8,128)S(1)}, f32[8,64,8]{1,2,0:T(8,128)}, u32[]{:S(2)}) copy-start(f32[8,64,8]{1,2,0:T(8,128)} %get-tuple-element.168) | copy-start | bytes 49156
  182.7 92.7 %collective-permute-start.1 = (f32[1,8,64,2,8,128]{5,4,3,2,1,0:T(8,128)}, f32[1,8,64,2,8,128]{5,4,3,2,1,0:T(8,128)}, u32[]{:S(2)}, u32[]{:S(2)}) collective-permute-start(f32[1,8,64,2,8,128]{5,4,3,2,1,0:T(8,128)} %copy.210), channel_id=1, source_target_pairs={{0,32},{8,40},{16,48},{24,56},{32,0},{40,8},{48,16},{56,24},{64,96... | collective-permute-start | bytes 12582920 | tf_op jit(solution)/shard_map/ppermute | solution.py:19
  306.8 8.4 %copy-start.1 = (f32[8,64,8,8]{1,2,3,0:T(8,128)S(1)}, f32[8,64,8,8]{1,2,3,0:T(8,128)}, u32[]{:S(2)}) copy-start(f32[8,64,8,8]{1,2,3,0:T(8,128)} %get-tuple-element.160) | copy-start | bytes 393220
  306.8 8.4 %copy-start = (f32[8,64,8,8]{1,2,3,0:T(8,128)S(1)}, f32[8,64,8,8]{1,2,3,0:T(8,128)}, u32[]{:S(2)}) copy-start(f32[8,64,8,8]{1,2,3,0:T(8,128)} %get-tuple-element.75) | copy-start | bytes 393220
  313.8 90.2 %collective-permute-start.2 = (f32[1,8,64,2,8,128]{5,4,3,2,1,0:T(8,128)}, f32[1,8,64,2,8,128]{5,4,3,2,1,0:T(8,128)}, u32[]{:S(2)}, u32[]{:S(2)}) collective-permute-start(f32[1,8,64,2,8,128]{5,4,3,2,1,0:T(8,128)} %copy.216), channel_id=1, source_target_pairs={{0,16},{8,24},{16,0},{24,8},{32,48},{40,56},{48,32},{56,40},{64,80... | collective-permute-start | bytes 12582920 | tf_op jit(solution)/shard_map/ppermute | solution.py:19
  445.5 10.1 %copy-start.4 = (s32[64]{0:T(128)S(1)}, s32[64]{0:T(128)}, u32[]{:S(2)}) copy-start(s32[64]{0:T(128)} %param.5) | copy-start | bytes 772
  452.3 19.0 %collective-permute-start.3 = (f32[1,8,64,2,8,128]{5,4,3,2,1,0:T(8,128)}, f32[1,8,64,2,8,128]{5,4,3,2,1,0:T(8,128)}, u32[]{:S(2)}, u32[]{:S(2)}) collective-permute-start(f32[1,8,64,2,8,128]{5,4,3,2,1,0:T(8,128)} %copy.229), channel_id=1, source_target_pairs={{0,8},{8,0},{16,24},{24,16},{32,40},{40,32},{48,56},{56,48},{64,72... | collective-permute-start | bytes 12582920 | tf_op jit(solution)/shard_map/ppermute | solution.py:19
where the time goes:
time: 578 us; the launch traced here: 570 us
  waiting for transfers between devices  202 us (35%)
  local copies, waits for them, and re-layouts  129 us (22%)
  other arithmetic  94.4 us (16%)
  matrix products  79.7 us (14%)
  blocking collectives  53.5 us (9%)
  starting transfers between devices  11.7 us (2%)
    ppermute x4, waiting for transfers between devices, swapped(): return lax.ppermute(value, axis, pairs)  202 us
    all_to_all x1, blocking collectives, local(): lax.all_to_all(ordered, 'narrow', split_axis=1, concat_axis=2, tiled=True)  53.5 us
    reshape x7, local copies, waits for them, and re-layouts, pull_child(): return moved.reshape(weights.shape)  48.5 us
    dot_general x4, matrix products, pull_child(): jnp.einsum('ab,...bcd->...acd', matrix, stacked, precision=lax.Precision....  42.7 us
    dot_general x4, matrix products, pull_child(): jnp.einsum('ab,...cbd->...cad', matrix, stacked, precision=lax.Precision....  37.1 us
    add x7, other arithmetic, pull_child(): turned_real = real_part * cosine + imag_part * sine_part  36.2 us
    add x4, other arithmetic, merge_partner(): return push_parent(retained + arrived, parent_angles)  29.8 us
    transpose x4, local copies, waits for them, and re-layouts, pull_child(): jnp.einsum('ab,...cbd->...cad', matrix, stacked, precision=lax.Precision....  21 us
  transfers between devices with their start and end apart: 4, of which 3 were waited for; matrix products, arithmetic and copies ran while one was open for 15% of the time, Pallas kernels for 0%

commit v1 on v0

v1 whole, which is shorter than its diff:
```python
import numpy as np
import jax
import jax.numpy as jnp
from jax import lax
from jax.experimental import pallas as pl
from jax.experimental.pallas import tpu as pltpu
from jax.sharding import PartitionSpec as P

SIN = (6.28318282, -41.3414214, 81.5961839, -76.5801007, 41.2053954, -12.2712631)
COS = (0.999999989, -19.7392045, 64.939119, -85.450166, 60.1678349, -25.9683235, 6.52962293)

NODES = 0.5 - 0.5 * np.cos(np.pi * (2.0 * np.arange(8) + 1.0) / 16.0)
TURNS = 16.0


def lagrange(child):
    points = (child + NODES) / 2.0
    out = np.ones((8, 8))
    for q in range(8):
        for m in range(8):
            if m != q:
                out[q] *= (points - NODES[m]) / (NODES[q] - NODES[m])
    return out


def turn(amount):
    return np.exp(2j * np.pi * TURNS * amount)


def dimension_operator(boxes):
    out = np.zeros((2, 2, 8, 2, 2, 8), complex)
    for ta in range(2):
        for tb in range(2):
            da, db = (2 * ta - 1) / 32.0, (2 * tb - 1) / 64.0
            last = turn((da + db) * 4.0 * NODES / boxes)
            for ca in range(2):
                for cb in range(2):
                    first = lagrange(ca) * turn(-da * (2 * cb + ca + NODES) / boxes)
                    second = lagrange(cb) * turn(-db * (2 * cb + 2 * NODES) / boxes)
                    out[ta, tb, :, ca, cb, :] = last[:, None] * (second @ first)
    return out


def halves(matrix):
    matrix = matrix.astype(np.float32)
    high = matrix.astype(jnp.bfloat16)
    low = (matrix - high.astype(np.float32)).astype(jnp.bfloat16)
    return high, low


def across_matrix():
    op = dimension_operator(64)
    real = np.zeros((2, 2, 2, 8, 2, 2, 2, 8))
    real[0, ..., 0, :] = op.real
    real[0, ..., 1, :] = -op.imag
    real[1, ..., 0, :] = op.imag
    real[1, ..., 1, :] = op.real
    high, low = halves(real.reshape(64, 64))
    return np.concatenate([high, high, low], axis=1)


def down_matrix():
    op = dimension_operator(16)
    real = np.zeros((2, 2, 2, 8, 2, 2, 2, 8))
    move = np.transpose(op, (3, 4, 5, 0, 1, 2))
    real[:, :, 0, :, 0] = move.real
    real[:, :, 1, :, 0] = -move.imag
    real[:, :, 0, :, 1] = move.imag
    real[:, :, 1, :, 1] = move.real
    flat = np.kron(real.reshape(64, 64), np.eye(16))
    return halves(flat)


def nodes_table():
    rows = np.repeat(NODES[:, None], 128, axis=1)
    lanes = np.repeat(np.repeat(NODES, 16)[None, :], 8, axis=0)
    return np.stack([rows, lanes]).astype(np.float32)


def horner(coefficients, x):
    total = jnp.full_like(x, coefficients[-1])
    for c in coefficients[-2::-1]:
        total = total * x + c
    return total


def unit(turns):
    rest = turns - jnp.round(turns)
    square = rest * rest
    return horner(COS, square), rest * horner(SIN, square)


def tables(nodes, super_index, first, second, count):
    sa = (super_index // 4).astype(jnp.float32)
    sd = (super_index % 4).astype(jnp.float32)
    local_a = first + count * nodes[0] - 2.0
    local_d = second + count * nodes[1] - 2.0
    mid_a, mid_d = 4.0 * sa + 2.0, 4.0 * sd + 2.0
    off_a, off_d = local_a / 64.0, local_d / 16.0
    key_a, key_d = (mid_a + local_a) / 64.0, (mid_d + local_d) / 16.0
    base_a, base_d = mid_a / 64.0, mid_d / 16.0
    key = jnp.sqrt(key_a * key_a + key_d * key_d)
    base = jnp.sqrt(jnp.zeros_like(key) + (base_a * base_a + base_d * base_d))
    radial = (off_a * (key_a + base_a) + off_d * (key_d + base_d)) / (key + base)
    return TURNS * off_a, TURNS * off_d, TURNS * radial


def turns_of(table, box, speed):
    center_a = ((box // 8).astype(jnp.float32) + 0.5) / 8.0
    center_d = ((box % 8).astype(jnp.float32) + 0.5) / 8.0
    return center_a * table[0] + center_d * table[1] + speed * table[2]


def pull_kernel(order_ref, speed_ref, nodes_ref, x_ref, o_ref):
    code = lax.axis_index("wide")
    super_index = lax.axis_index("narrow") * 8 + pl.program_id(0)
    bits = [(code >> k & 1).astype(jnp.float32) for k in range(4)]
    table = tables(nodes_ref, super_index, 2.0 * bits[1] + bits[3], 2.0 * bits[0] + bits[2], 1.0)

    def slot(place, carry):
        j = place // 4 % 8 * 8 + place // 32 * 4 + place % 4
        box = order_ref[j]
        cosine, sine = unit(turns_of(table, box, speed_ref[box]))
        real, imag = x_ref[0, box, 0], x_ref[0, box, 1]
        o_ref[0, place, 0] = real * cosine + imag * sine
        o_ref[0, place, 1] = imag * cosine - real * sine
        return carry

    lax.fori_loop(0, 64, slot, 0, unroll=8)


def split(value):
    high = value.astype(jnp.bfloat16)
    return high, (value - high.astype(jnp.float32)).astype(jnp.bfloat16)


def merge_kernel(pairs, order_ref, speed_ref, nodes_ref, across_ref, high_ref, low_ref, x_ref, o_ref, rows_h, rows_l):
    place = lax.axis_index("wide")
    super_index = lax.axis_index("narrow") * 8 + place // 2
    half = place % 2
    table = tables(nodes_ref, super_index, 0.0, 0.0, 4.0)
    across = across_ref[...]
    for g2 in range(2):
        for g0 in range(2):
            columns = []
            for p in range(pairs):
                parts = [x_ref[8 * g3 + 4 * g2 + 2 * g1 + g0, p].reshape(16, 128) for g3 in range(2) for g1 in range(2)]
                columns.append(jnp.concatenate(parts, axis=0))
            high, low = split(jnp.concatenate(columns, axis=1))
            moved = jnp.dot(across, jnp.concatenate([high, low, high], axis=0), preferred_element_type=jnp.float32)
            high, low = split(moved)
            for u in range(2):
                lane = 128 * (4 * g2 + 2 * g0 + u)
                for p in range(pairs):
                    rows_h[32 * p : 32 * p + 32, lane : lane + 128] = high[32 * u : 32 * u + 32, 128 * p : 128 * p + 128]
                    rows_l[32 * p : 32 * p + 32, lane : lane + 128] = low[32 * u : 32 * u + 32, 128 * p : 128 * p + 128]
    lanes = []
    for t2 in range(2):
        for t0 in range(2):
            result = []
            for u in range(2):
                lane = 128 * (4 * u + 2 * t2 + t0)
                wh, wl = high_ref[:, lane : lane + 128], low_ref[:, lane : lane + 128]
                result.append((wh, wl))
            wh = jnp.concatenate([result[0][0], result[1][0]], axis=1)
            wl = jnp.concatenate([result[0][1], result[1][1]], axis=1)
            total = jnp.dot(rows_h[...], wh, preferred_element_type=jnp.float32)
            total += jnp.dot(rows_l[...], wh, preferred_element_type=jnp.float32)
            total += jnp.dot(rows_h[...], wl, preferred_element_type=jnp.float32)
            lanes.append(total)
    for p in range(pairs):
        slot = pl.program_id(0) * pairs + p
        box = order_ref[slot // 4 * 8 + half * 4 + slot % 4]
        cosine, sine = unit(turns_of(table, box, speed_ref[box]))
        for t2 in range(2):
            for t0 in range(2):
                for t3 in range(2):
                    for t1 in range(2):
                        at = 32 * p + 16 * t3 + 8 * t1
                        block = lanes[2 * t2 + t0][at : at + 8]
                        real, imag = block[:, :128], block[:, 128:]
                        t = 8 * t3 + 4 * t2 + 2 * t1 + t0
                        o_ref[t, p, 0] = real * cosine - imag * sine
                        o_ref[t, p, 1] = real * sine + imag * cosine


SMEM = pl.BlockSpec(memory_space=pltpu.SMEM)


def whole(shape):
    return pl.BlockSpec(shape, lambda i: (0,) * len(shape))


def pull(order, speed, x):
    block = pl.BlockSpec((1, 64, 2, 8, 128), lambda i: (i, 0, 0, 0, 0))
    return pl.pallas_call(
        pull_kernel,
        grid=(8,),
        out_shape=jax.ShapeDtypeStruct((8, 64, 2, 8, 128), jnp.float32),
        in_specs=[SMEM, SMEM, whole((2, 8, 128)), block],
        out_specs=block,
        compiler_params=pltpu.CompilerParams(vmem_limit_bytes=32 * 2**20),
    )(order, speed, nodes_table(), x)


def merge(order, speed, x, pairs=16):
    high, low = down_matrix()
    block = pl.BlockSpec((16, pairs, 2, 8, 128), lambda i: (0, i, 0, 0, 0))
    return pl.pallas_call(
        lambda *refs: merge_kernel(pairs, *refs),
        grid=(32 // pairs,),
        out_shape=jax.ShapeDtypeStruct((16, 32, 2, 8, 128), jnp.float32),
        in_specs=[SMEM, SMEM, whole((2, 8, 128)), whole((64, 192)), whole((1024, 1024)), whole((1024, 1024)), block],
        out_specs=block,
        scratch_shapes=[pltpu.VMEM((32 * pairs, 1024), jnp.bfloat16)] * 2,
        compiler_params=pltpu.CompilerParams(vmem_limit_bytes=48 * 2**20),
    )(order, speed, nodes_table(), across_matrix(), high, low, x)


def local(weights_in, medium_speed, target_order):
    speed = medium_speed.reshape(-1)
    turned = pull(target_order, speed, weights_in[0])
    gathered = lax.all_to_all(turned.reshape(16, 32, 2, 8, 128), "wide", 0, 0)
    merged = merge(target_order, speed, gathered)
    spread = lax.all_to_all(merged.reshape(128, 4, 2, 8, 128), ("wide", "narrow"), 0, 0, tiled=True)
    spread = spread.reshape(8, 2, 8, 4, 2, 8, 128)
    return jnp.transpose(spread, (1, 3, 2, 0, 4, 5, 6)).reshape(1, 8, 64, 2, 8, 128)


def solution(mesh):
    in_specs = (P("wide", "narrow", None, None, None, None), P(), P())
    out_specs = P("wide", "narrow", None, None, None, None)
    return jax.shard_map(local, mesh=mesh, in_specs=in_specs, out_specs=out_specs, check_vma=False)
```

time: 578 us -> 149 us (0.26); the launches traced: 570 us -> 148 us
  waiting for transfers between devices: 202 us -> 0 us
  local copies, waits for them, and re-layouts: 129 us -> 6.97 us
  other arithmetic: 94.4 us -> 0 us
  matrix products: 79.7 us -> 0 us
  blocking collectives: 53.5 us -> 117 us
  Pallas kernels: 0 us -> 23.4 us
  starting transfers between devices: 11.7 us -> 0 us
    ppermute x4 -> x0, waiting for transfers between devices: 202 us -> none  [swapped(): return lax.ppermute(value, axis, pairs)]
    dot_general x8 -> x0, matrix products: 79.7 us -> none  [the longest x4 42.7 us: pull_child(): jnp.einsum('ab,...bcd->...acd', matrix, stacked, precision=lax.Precision....]
    add x11 -> x0, other arithmetic: 66 us -> none  [the longest x7 36.2 us: pull_child(): turned_real = real_part * cosine + imag_part * sine_part]
    all_to_all x1 -> x2, blocking collectives: 53.5 us -> 117 us  [the longest x1 60.2 us: local(): gathered = lax.all_to_all(turned.reshape(16, 32, 2, 8, 128), 'wide', 0, 0)]
    reshape x8 -> x2, local copies, waits for them, and re-layouts: 55.4 us -> 3.39 us  [the longest x1 2.63 us: local(): spread = spread.reshape(8, 2, 8, 4, 2, 8, 128)]
    pallas_call x0 -> x2, Pallas kernels: none -> 23.4 us  [the longest x1 11.9 us: pull(): pl.pallas_call(pull_kernel, grid=(8,), out_shape=jax.ShapeDtypeStruct((8,...]
    transpose x4 -> x0, local copies, waits for them, and re-layouts: 21 us -> none  [pull_child(): jnp.einsum('ab,...cbd->...cad', matrix, stacked, precision=lax.Precision....]
    add x2 -> x0, local copies, waits for them, and re-layouts: 14 us -> none  [merge_partner(): return push_parent(retained + arrived, parent_angles)]
  transfers between devices with their start and end apart: 4 -> 0, of which waited for: 3 -> 0; matrix products, arithmetic and copies ran while one was open for 15% -> 0% of each run, Pallas kernels for 0% -> 0%
where the time goes in v1:
time: 149 us; the launch traced here: 148 us
  blocking collectives  117 us (79%)
  Pallas kernels  23.4 us (16%)
  local copies, waits for them, and re-layouts  6.97 us (5%)
    all_to_all x1, blocking collectives, local(): gathered = lax.all_to_all(turned.reshape(16, 32, 2, 8, 128), 'wide', 0, 0)  60.2 us
    all_to_all x1, blocking collectives, local(): lax.all_to_all(merged.reshape(128, 4, 2, 8, 128), ('wide', 'narrow'), 0,...  57.3 us
    pallas_call x1, Pallas kernels, pull(): pl.pallas_call(pull_kernel, grid=(8,), out_shape=jax.ShapeDtypeStruct((8,...  11.9 us
    pallas_call x1, Pallas kernels, merge(): pl.pallas_call(lambda *refs: merge_kernel(pairs, *refs), grid=(32 // pair...  11.5 us
    unnamed x16, local copies, waits for them, and re-layouts  3.58 us

profile of v1, /device:TPU:1, one launch (start us, length us, event | category | flops | bytes accessed | tf_op | source)
XLA Modules:
  0.0 147.8 jit_solution(4095233307663318204)
XLA Ops:
  0.0 0.8 reshape.15.speed_ref.refs_1_
  0.8 0.0 copy-start
  0.8 2.2 %copy-done = f32[1,8,64,2,8,128]{5,4,3,2,1,0:T(8,128)S(1)} copy-done((f32[1,8,64,2,8,128]{5,4,3,2,1,0:T(8,128)S(1)}, f32[1,8,64,2,8,128]{5,4,3,2,1,0:T(8,128)}, u32[]{:S(2)}) %copy-start) | copy-done | bytes 4194328
  3.0 0.0 copy-start.4
  3.0 0.7 copy-done.4
  3.7 0.0 copy-start.6
  3.7 0.7 copy-done.6
  4.3 11.9 %shard_map.82 = f32[8,64,2,8,128]{4,3,2,1,0:T(8,128)S(1)} custom-call(s32[64]{0:T(128)S(1)} %copy-done.6, f32[64]{0:T(128)S(1)} %reshape.15.speed_ref.refs_1_, f32[2,8,128]{2,1,0:T(8,128)S(1)} %copy-done.4, f32[8,64,2,8,128]{4,3,2,1,0:T(8,128)S(1)} %bitcast.8), custom_call_target="tpu_custom_call" | custom-call | tf_op jit(solution)/shard_map/pallas_call | solution.py:196
  16.2 0.0 copy-start.1
  16.2 0.0 copy-start.2
  16.2 0.0 copy-start.3
  16.2 0.0 copy-start.5
  16.2 0.0 copy-start.7
  16.2 60.2 %all_to_all.10.refs_6_ = f32[16,32,2,8,128]{4,3,2,1,0:T(8,128)} all-to-all(f32[16,32,2,8,128]{4,3,2,1,0:T(8,128)S(1)} %bitcast.7), channel_id=1, replica_groups=mesh['wide'=16,'narrow'=8] {'wide'}, dimensions={0} | all-to-all | bytes 8388608 | tf_op jit(solution)/shard_map/all_to_all | solution.py:223
  76.4 0.0 copy-done.1
  76.4 0.0 copy-done.2
  76.4 0.0 copy-done.3
  76.4 0.0 copy-done.5
  76.4 0.0 copy-done.7
  76.4 11.5 %shard_map.83 = f32[16,32,2,8,128]{4,3,2,1,0:T(8,128)} custom-call(s32[64]{0:T(128)S(1)} %copy-done.7, f32[64]{0:T(128)S(1)} %reshape.15.speed_ref.refs_1_, f32[2,8,128]{2,1,0:T(8,128)S(1)} %copy-done.5, bf16[64,192]{1,0:T(8,128)(2,1)S(1)} %copy-done.3, bf16[1024,1024]{1,0:T(8,128)(2,1)S(1)} %copy-done.2, bf16[1024,1024]{1,0:T(8,128)(2,1)S(1)} %copy-done.1, ...), custom_call_target="tpu_custom_call" | custom-call | tf_op jit(solution)/shard_map/pallas_call | solution.py:209
  87.9 57.3 %all_to_all.11 = f32[128,4,2,8,128]{4,3,2,1,0:T(8,128)S(1)} all-to-all(f32[128,4,2,8,128]{4,3,2,1,0:T(8,128)} %bitcast.10), channel_id=1, replica_groups=mesh['wide'=16,'narrow'=8] {'wide','narrow'}, dimensions={0} | all-to-all | bytes 8388608 | tf_op jit(solution)/shard_map/all_to_all | solution.py:225
  145.2 2.6 %copy.9 = f32[8,2,8,4,2,8,128]{6,5,4,0,2,3,1:T(8,128)} copy(f32[8,2,8,4,2,8,128]{6,5,4,3,2,1,0:T(8,128)S(1)} %bitcast.9) | data formatting | bytes 8388608 | tf_op jit(solution)/shard_map/reshape | solution.py:226
Async XLA Ops:
  0.8 2.2 %copy-start = (f32[1,8,64,2,8,128]{5,4,3,2,1,0:T(8,128)S(1)}, f32[1,8,64,2,8,128]{5,4,3,2,1,0:T(8,128)}, u32[]{:S(2)}) copy-start(f32[1,8,64,2,8,128]{5,4,3,2,1,0:T(8,128)} %param.8) | copy-start | bytes 12582916
  3.0 0.7 copy-start.4
  3.7 0.7 copy-start.6
  16.2 60.2 %copy-start.1 = (bf16[1024,1024]{1,0:T(8,128)(2,1)S(1)}, bf16[1024,1024]{1,0:T(8,128)(2,1)}, u32[]{:S(2)}) copy-start(bf16[1024,1024]{1,0:T(8,128)(2,1)} %constant.11.clone.refs_5_) | copy-start | bytes 6291460
  16.2 60.2 %copy-start.2 = (bf16[1024,1024]{1,0:T(8,128)(2,1)S(1)}, bf16[1024,1024]{1,0:T(8,128)(2,1)}, u32[]{:S(2)}) copy-start(bf16[1024,1024]{1,0:T(8,128)(2,1)} %constant.10.clone.refs_4_) | copy-start | bytes 6291460
  16.2 60.2 %copy-start.3 = (bf16[64,192]{1,0:T(8,128)(2,1)S(1)}, bf16[64,192]{1,0:T(8,128)(2,1)}, u32[]{:S(2)}) copy-start(bf16[64,192]{1,0:T(8,128)(2,1)} %constant.9.clone.refs_3_) | copy-start | bytes 73732
  16.2 60.2 %copy-start.5 = (f32[2,8,128]{2,1,0:T(8,128)S(1)}, f32[2,8,128]{2,1,0:T(8,128)}, u32[]{:S(2)}) copy-start(f32[2,8,128]{2,1,0:T(8,128)} %constant.8.clone.nodes_ref.refs_2_) | copy-start | bytes 24580
  16.2 60.2 %copy-start.7 = (s32[64]{0:T(128)S(1)}, s32[64]{0:T(128)}, u32[]{:S(2)}) copy-start(s32[64]{0:T(128)} %refs_0_.1) | copy-start | bytes 772

commit v2 on v1

--- a/solution.py
+++ b/solution.py
@@ -11,6 +11,7 @@
 
 NODES = 0.5 - 0.5 * np.cos(np.pi * (2.0 * np.arange(8) + 1.0) / 16.0)
 TURNS = 16.0
+SUPERS = 4
 
 
 def lagrange(child):
@@ -71,10 +72,12 @@
     return halves(flat)
 
 
-def nodes_table():
-    rows = np.repeat(NODES[:, None], 128, axis=1)
-    lanes = np.repeat(np.repeat(NODES, 16)[None, :], 8, axis=0)
-    return np.stack([rows, lanes]).astype(np.float32)
+def spread_matrix():
+    one = np.zeros((16, 8, 16, 8, 16))
+    for box in range(16):
+        one[box, np.arange(8), box, np.arange(8)] = 1.0
+    one = one.reshape(128, 2048)
+    return np.concatenate([one, one]).astype(jnp.bfloat16)
 
 
 def horner(coefficients, x):
@@ -90,11 +93,22 @@
     return horner(COS, square), rest * horner(SIN, square)
 
 
-def tables(nodes, super_index, first, second, count):
+def node_at(index):
+    value = jnp.full(index.shape, NODES[0], jnp.float32)
+    for q in range(1, 8):
+        value = jnp.where(index == q, jnp.float32(NODES[q]), value)
+    return value
+
+
+def iota(axis):
+    return lax.broadcasted_iota(jnp.int32, (8, 128), axis)
+
+
+def tables(node_a, node_d, super_index, first, second, count):
     sa = (super_index // 4).astype(jnp.float32)
     sd = (super_index % 4).astype(jnp.float32)
-    local_a = first + count * nodes[0] - 2.0
-    local_d = second + count * nodes[1] - 2.0
+    local_a = first + count * node_a - 2.0
+    local_d = second + count * node_d - 2.0
     mid_a, mid_d = 4.0 * sa + 2.0, 4.0 * sd + 2.0
     off_a, off_d = local_a / 64.0, local_d / 16.0
     key_a, key_d = (mid_a + local_a) / 64.0, (mid_d + local_d) / 16.0
@@ -105,28 +119,55 @@
     return TURNS * off_a, TURNS * off_d, TURNS * radial
 
 
-def turns_of(table, box, speed):
-    center_a = ((box // 8).astype(jnp.float32) + 0.5) / 8.0
-    center_d = ((box % 8).astype(jnp.float32) + 0.5) / 8.0
-    return center_a * table[0] + center_d * table[1] + speed * table[2]
-
-
-def pull_kernel(order_ref, speed_ref, nodes_ref, x_ref, o_ref):
-    code = lax.axis_index("wide")
-    super_index = lax.axis_index("narrow") * 8 + pl.program_id(0)
-    bits = [(code >> k & 1).astype(jnp.float32) for k in range(4)]
-    table = tables(nodes_ref, super_index, 2.0 * bits[1] + bits[3], 2.0 * bits[0] + bits[2], 1.0)
-
-    def slot(place, carry):
-        j = place // 4 % 8 * 8 + place // 32 * 4 + place % 4
-        box = order_ref[j]
-        cosine, sine = unit(turns_of(table, box, speed_ref[box]))
-        real, imag = x_ref[0, box, 0], x_ref[0, box, 1]
-        o_ref[0, place, 0] = real * cosine + imag * sine
-        o_ref[0, place, 1] = imag * cosine - real * sine
-        return carry
-
-    lax.fori_loop(0, 64, slot, 0, unroll=8)
+def fetch(order_hbm, speed_hbm, order_ref, speed_ref, sems):
+    copies = [
+        pltpu.make_async_copy(order_hbm, order_ref, sems.at[0]),
+        pltpu.make_async_copy(speed_hbm, speed_ref, sems.at[1]),
+    ]
+    for copy in copies:
+        copy.start()
+    for copy in copies:
+        copy.wait()
+
+
+def pull_kernel(order_hbm, speed_hbm, spread_ref, x_ref, o_ref, order_ref, speed_ref, place_ref, turned, sems):
+    @pl.when(pl.program_id(0) == 0)
+    def _():
+        fetch(order_hbm, speed_hbm, order_ref, speed_ref, sems)
+        for j in range(64):
+            place_ref[order_ref[j]] = j % 8 // 4 * 32 + j // 8 * 4 + j % 4
+        code = lax.axis_index("wide")
+        bits = [(code >> k & 1).astype(jnp.float32) for k in range(4)]
+        lane = iota(1)
+        node_a, node_d = node_at(iota(0)), node_at(lane % 8)
+        center_d = (lane // 8 % 8).astype(jnp.float32) / 8.0 + 0.0625
+        center_a, speed = [], []
+        for high in range(4):
+            center_a.append((lane // 64 + 2 * high).astype(jnp.float32) / 8.0 + 0.0625)
+            value = jnp.zeros((8, 128), jnp.float32)
+            for low in range(16):
+                value = jnp.where(lane // 8 == low, speed_ref[2 * high + low // 8, low % 8], value)
+            speed.append(value)
+        for s in range(8):
+            super_index = lax.axis_index("narrow") * 8 + s
+            table = tables(node_a, node_d, super_index, 2.0 * bits[1] + bits[3], 2.0 * bits[0] + bits[2], 1.0)
+            turns = [center_a[h] * table[0] + (center_d * table[1] + speed[h] * table[2]) for h in range(4)]
+            cosine, sine = unit(jnp.concatenate(turns, axis=0))
+            high, low = split(jnp.concatenate([cosine, sine], axis=0))
+            turned[s] = jnp.dot(
+                jnp.concatenate([high, low], axis=1), spread_ref[...], preferred_element_type=jnp.float32
+            )
+
+    for s in range(SUPERS):
+        at_super = pl.program_id(0) * SUPERS + s
+        for box in range(64):
+            place = place_ref[box]
+            at, lane = 8 * (box // 16), 128 * (box % 16)
+            cosine = turned[at_super, at : at + 8, lane : lane + 128]
+            sine = turned[at_super, 32 + at : 40 + at, lane : lane + 128]
+            real, imag = x_ref[s, box, 0], x_ref[s, box, 1]
+            o_ref[s, place, 0] = real * cosine + imag * sine
+            o_ref[s, place, 1] = imag * cosine - real * sine
 
 
 def split(value):
@@ -134,11 +175,17 @@
     return high, (value - high.astype(jnp.float32)).astype(jnp.bfloat16)
 
 
-def merge_kernel(pairs, order_ref, speed_ref, nodes_ref, across_ref, high_ref, low_ref, x_ref, o_ref, rows_h, rows_l):
+def merge_kernel(
+    pairs, order_hbm, speed_hbm, across_ref, high_ref, low_ref, x_ref, o_ref, order_ref, speed_ref, rows_h, rows_l, sems
+):
+    @pl.when(pl.program_id(0) == 0)
+    def _():
+        fetch(order_hbm, speed_hbm, order_ref, speed_ref, sems)
+
     place = lax.axis_index("wide")
     super_index = lax.axis_index("narrow") * 8 + place // 2
     half = place % 2
-    table = tables(nodes_ref, super_index, 0.0, 0.0, 4.0)
+    table = tables(node_at(iota(0)), node_at(iota(1) // 16), super_index, 0.0, 0.0, 4.0)
     across = across_ref[...]
     for g2 in range(2):
         for g0 in range(2):
@@ -171,7 +218,10 @@
     for p in range(pairs):
         slot = pl.program_id(0) * pairs + p
         box = order_ref[slot // 4 * 8 + half * 4 + slot % 4]
-        cosine, sine = unit(turns_of(table, box, speed_ref[box]))
+        center_a = (box // 8).astype(jnp.float32) / 8.0 + 0.0625
+        center_d = (box % 8).astype(jnp.float32) / 8.0 + 0.0625
+        turns = center_a * table[0] + (center_d * table[1] + speed_ref[box // 8, box % 8] * table[2])
+        cosine, sine = unit(turns)
         for t2 in range(2):
             for t0 in range(2):
                 for t3 in range(2):
@@ -184,7 +234,8 @@
                         o_ref[t, p, 1] = real * sine + imag * cosine
 
 
-SMEM = pl.BlockSpec(memory_space=pltpu.SMEM)
+ANY = pl.BlockSpec(memory_space=pl.ANY)
+LOOKUP = [pltpu.SMEM((64,), jnp.int32), pltpu.SMEM((8, 8), jnp.float32)]
 
 
 def whole(shape):
@@ -192,15 +243,17 @@
 
 
 def pull(order, speed, x):
-    block = pl.BlockSpec((1, 64, 2, 8, 128), lambda i: (i, 0, 0, 0, 0))
+    block = pl.BlockSpec((SUPERS, 64, 2, 8, 128), lambda i: (i, 0, 0, 0, 0))
     return pl.pallas_call(
         pull_kernel,
-        grid=(8,),
+        grid=(8 // SUPERS,),
         out_shape=jax.ShapeDtypeStruct((8, 64, 2, 8, 128), jnp.float32),
-        in_specs=[SMEM, SMEM, whole((2, 8, 128)), block],
+        in_specs=[ANY, ANY, whole((256, 2048)), block],
         out_specs=block,
-        compiler_params=pltpu.CompilerParams(vmem_limit_bytes=32 * 2**20),
-    )(order, speed, nodes_table(), x)
+        scratch_shapes=LOOKUP
+        + [pltpu.SMEM((64,), jnp.int32), pltpu.VMEM((8, 64, 2048), jnp.float32), pltpu.SemaphoreType.DMA((2,))],
+        compiler_params=pltpu.CompilerParams(vmem_limit_bytes=60 * 2**20),
+    )(order, speed, spread_matrix(), x)
 
 
 def merge(order, speed, x, pairs=16):
@@ -210,18 +263,17 @@
         lambda *refs: merge_kernel(pairs, *refs),
         grid=(32 // pairs,),
         out_shape=jax.ShapeDtypeStruct((16, 32, 2, 8, 128), jnp.float32),
-        in_specs=[SMEM, SMEM, whole((2, 8, 128)), whole((64, 192)), whole((1024, 1024)), whole((1024, 1024)), block],
+        in_specs=[ANY, ANY, whole((64, 192)), whole((1024, 1024)), whole((1024, 1024)), block],
         out_specs=block,
-        scratch_shapes=[pltpu.VMEM((32 * pairs, 1024), jnp.bfloat16)] * 2,
+        scratch_shapes=LOOKUP + [pltpu.VMEM((32 * pairs, 1024), jnp.bfloat16)] * 2 + [pltpu.SemaphoreType.DMA((2,))],
         compiler_params=pltpu.CompilerParams(vmem_limit_bytes=48 * 2**20),
-    )(order, speed, nodes_table(), across_matrix(), high, low, x)
+    )(order, speed, across_matrix(), high, low, x)
 
 
 def local(weights_in, medium_speed, target_order):
-    speed = medium_speed.reshape(-1)
-    turned = pull(target_order, speed, weights_in[0])
+    turned = pull(target_order, medium_speed, weights_in[0])
     gathered = lax.all_to_all(turned.reshape(16, 32, 2, 8, 128), "wide", 0, 0)
-    merged = merge(target_order, speed, gathered)
+    merged = merge(target_order, medium_speed, gathered)
     spread = lax.all_to_all(merged.reshape(128, 4, 2, 8, 128), ("wide", "narrow"), 0, 0, tiled=True)
     spread = spread.reshape(8, 2, 8, 4, 2, 8, 128)
     return jnp.transpose(spread, (1, 3, 2, 0, 4, 5, 6)).reshape(1, 8, 64, 2, 8, 128)

time: 149 us -> 140 us (0.940)
  Pallas kernels: 23.4 us -> 18.6 us
  local copies, waits for them, and re-layouts: 6.97 us -> 2.66 us
    pallas_call x1, Pallas kernels: 11.9 us -> 6.51 us  [pull(): pl.pallas_call(pull_kernel, grid=(8 // SUPERS,), out_shape=jax.ShapeDtype...]
    unnamed x16 -> x10, local copies, waits for them, and re-layouts: 3.58 us -> 0.03 us
where the time goes in v2:
time: 140 us; the launch traced here: 139 us
  blocking collectives  118 us (84%)
  Pallas kernels  18.6 us (13%)
  local copies, waits for them, and re-layouts  2.66 us (2%)
    all_to_all x1, blocking collectives, local(): gathered = lax.all_to_all(turned.reshape(16, 32, 2, 8, 128), 'wide', 0, 0)  60.4 us
    all_to_all x1, blocking collectives, local(): lax.all_to_all(merged.reshape(128, 4, 2, 8, 128), ('wide', 'narrow'), 0,...  57.3 us
    pallas_call x1, Pallas kernels, merge(): pl.pallas_call(lambda *refs: merge_kernel(pairs, *refs), grid=(32 // pair...  12.1 us
    pallas_call x1, Pallas kernels, pull(): pl.pallas_call(pull_kernel, grid=(8 // SUPERS,), out_shape=jax.ShapeDtype...  6.51 us

profile of v2, /device:TPU:1, one launch (start us, length us, event | category | flops | bytes accessed | tf_op | source)
XLA Modules:
  0.0 139.0 jit_solution(15604784341970516492)
XLA Ops:
  0.0 6.5 %shard_map.73 = f32[8,64,2,8,128]{4,3,2,1,0:T(8,128)} custom-call(s32[64]{0:T(128)} %refs_0_.1, f32[8,8]{1,0:T(8,128)} %refs_1_.1, bf16[256,2048]{1,0:T(8,128)(2,1)} %constant.8.clone.spread_ref, f32[8,64,2,8,128]{4,3,2,1,0:T(8,128)} %bitcast.10), custom_call_target="tpu_custom_call" | custom-call | tf_op jit(solution)/shard_map/pallas_call | solution.py:247
  6.5 0.0 copy-start
  6.5 0.0 copy-start.1
  6.5 0.0 copy-start.2
  6.6 0.0 copy-start.3
  6.6 0.0 copy-start.4
  6.6 60.4 %all_to_all.10.refs_5_ = f32[16,32,2,8,128]{4,3,2,1,0:T(8,128)} all-to-all(f32[16,32,2,8,128]{4,3,2,1,0:T(8,128)} %bitcast.8), channel_id=1, replica_groups=mesh['wide'=16,'narrow'=8] {'wide'}, dimensions={0} | all-to-all | bytes 8388608 | tf_op jit(solution)/shard_map/all_to_all | solution.py:275
  67.0 0.0 copy-done
  67.0 0.0 copy-done.1
  67.0 0.0 copy-done.2
  67.0 0.0 copy-done.3
  67.0 0.0 copy-done.4
  67.0 12.1 %shard_map.74 = f32[16,32,2,8,128]{4,3,2,1,0:T(8,128)} custom-call(s32[64]{0:T(128)S(1)} %copy-done.4, f32[8,8]{1,0:T(8,128)S(1)} %copy-done.3, bf16[64,192]{1,0:T(8,128)(2,1)S(1)} %copy-done.2, bf16[1024,1024]{1,0:T(8,128)(2,1)S(1)} %copy-done.1, bf16[1024,1024]{1,0:T(8,128)(2,1)S(1)} %copy-done, f32[16,32,2,8,128]{4,3,2,1,0:T(8,128)} %all_to_all.10.refs_5_), custom_call_target="tpu_custom_call" | custom-call | tf_op jit(solution)/shard_map/pallas_call | solution.py:262
  79.1 57.3 %all_to_all.11 = f32[128,4,2,8,128]{4,3,2,1,0:T(8,128)S(1)} all-to-all(f32[128,4,2,8,128]{4,3,2,1,0:T(8,128)} %bitcast.7), channel_id=1, replica_groups=mesh['wide'=16,'narrow'=8] {'wide','narrow'}, dimensions={0} | all-to-all | bytes 8388608 | tf_op jit(solution)/shard_map/all_to_all | solution.py:277
  136.4 2.6 %copy.8 = f32[8,2,8,4,2,8,128]{6,5,4,0,2,3,1:T(8,128)} copy(f32[8,2,8,4,2,8,128]{6,5,4,3,2,1,0:T(8,128)S(1)} %bitcast.9) | data formatting | bytes 8388608 | tf_op jit(solution)/shard_map/reshape | solution.py:278
Async XLA Ops:
  6.5 60.5 %copy-start = (bf16[1024,1024]{1,0:T(8,128)(2,1)S(1)}, bf16[1024,1024]{1,0:T(8,128)(2,1)}, u32[]{:S(2)}) copy-start(bf16[1024,1024]{1,0:T(8,128)(2,1)} %constant.11.clone.refs_4_) | copy-start | bytes 6291460
  6.5 60.4 %copy-start.1 = (bf16[1024,1024]{1,0:T(8,128)(2,1)S(1)}, bf16[1024,1024]{1,0:T(8,128)(2,1)}, u32[]{:S(2)}) copy-start(bf16[1024,1024]{1,0:T(8,128)(2,1)} %constant.10.clone.refs_3_) | copy-start | bytes 6291460
  6.5 60.4 %copy-start.2 = (bf16[64,192]{1,0:T(8,128)(2,1)S(1)}, bf16[64,192]{1,0:T(8,128)(2,1)}, u32[]{:S(2)}) copy-start(bf16[64,192]{1,0:T(8,128)(2,1)} %constant.9.clone.refs_2_) | copy-start | bytes 73732
  6.6 60.4 %copy-start.3 = (f32[8,8]{1,0:T(8,128)S(1)}, f32[8,8]{1,0:T(8,128)}, u32[]{:S(2)}) copy-start(f32[8,8]{1,0:T(8,128)} %refs_1_.1) | copy-start | bytes 772
  6.6 60.4 %copy-start.4 = (s32[64]{0:T(128)S(1)}, s32[64]{0:T(128)}, u32[]{:S(2)}) copy-start(s32[64]{0:T(128)} %refs_0_.1) | copy-start | bytes 772

commit v3 on v2

v3 whole, which is shorter than its diff:
```python
import numpy as np
import jax
import jax.numpy as jnp
from jax import lax
from jax.experimental import pallas as pl
from jax.experimental.pallas import tpu as pltpu
from jax.sharding import Mesh, PartitionSpec as P

SIN = (6.28318282, -41.3414214, 81.5961839, -76.5801007, 41.2053954, -12.2712631)
COS = (0.999999989, -19.7392045, 64.939119, -85.450166, 60.1678349, -25.9683235, 6.52962293)

NODES = 0.5 - 0.5 * np.cos(np.pi * (2.0 * np.arange(8) + 1.0) / 16.0)
TURNS = 16.0
FINE = ("z_hi", "y", "core", "z_lo", "x")
FINE_SIZES = (2, 4, 2, 2, 4)
WIDE, NARROW = FINE[:3], FINE[3:]


def lagrange(child):
    points = (child + NODES) / 2.0
    out = np.ones((8, 8))
    for q in range(8):
        for m in range(8):
            if m != q:
                out[q] *= (points - NODES[m]) / (NODES[q] - NODES[m])
    return out


def turn(amount):
    return np.exp(2j * np.pi * TURNS * amount)


def dimension_operator(boxes):
    out = np.zeros((2, 2, 8, 2, 2, 8), complex)
    for ta in range(2):
        for tb in range(2):
            da, db = (2 * ta - 1) / 32.0, (2 * tb - 1) / 64.0
            last = turn((da + db) * 4.0 * NODES / boxes)
            for ca in range(2):
                for cb in range(2):
                    first = lagrange(ca) * turn(-da * (2 * cb + ca + NODES) / boxes)
                    second = lagrange(cb) * turn(-db * (2 * cb + 2 * NODES) / boxes)
                    out[ta, tb, :, ca, cb, :] = last[:, None] * (second @ first)
    return out


def halves(matrix):
    matrix = matrix.astype(np.float32)
    high = matrix.astype(jnp.bfloat16)
    low = (matrix - high.astype(np.float32)).astype(jnp.bfloat16)
    return high, low


def across_matrix():
    op = dimension_operator(64)
    real = np.zeros((2, 2, 2, 8, 2, 2, 2, 8))
    real[0, ..., 0, :] = op.real
    real[0, ..., 1, :] = -op.imag
    real[1, ..., 0, :] = op.imag
    real[1, ..., 1, :] = op.real
    high, low = halves(real.reshape(64, 64))
    return np.concatenate([high, high, low], axis=1)


def down_matrix():
    move = np.transpose(dimension_operator(16), (3, 4, 5, 0, 1, 2))[:, :, :, 0]
    real = np.stack([move.real, move.imag], axis=4)
    return halves(np.kron(real.reshape(32, 32), np.eye(16)))


def spread_matrix():
    one = np.zeros((16, 8, 16, 8, 16))
    for box in range(16):
        one[box, np.arange(8), box, np.arange(8)] = 1.0
    one = one.reshape(128, 2048)
    return np.concatenate([one, one]).astype(jnp.bfloat16)


def horner(coefficients, x):
    total = jnp.full_like(x, coefficients[-1])
    for c in coefficients[-2::-1]:
        total = total * x + c
    return total


def unit(turns):
    rest = turns - jnp.round(turns)
    square = rest * rest
    return horner(COS, square), rest * horner(SIN, square)


def node_at(index):
    value = jnp.full(index.shape, NODES[0], jnp.float32)
    for q in range(1, 8):
        value = jnp.where(index == q, jnp.float32(NODES[q]), value)
    return value


def iota(axis):
    return lax.broadcasted_iota(jnp.int32, (8, 128), axis)


def tables(node_a, node_d, super_index, first, second, count):
    sa = (super_index // 4).astype(jnp.float32)
    sd = (super_index % 4).astype(jnp.float32)
    local_a = first + count * node_a - 2.0
    local_d = second + count * node_d - 2.0
    mid_a, mid_d = 4.0 * sa + 2.0, 4.0 * sd + 2.0
    off_a, off_d = local_a / 64.0, local_d / 16.0
    key_a, key_d = (mid_a + local_a) / 64.0, (mid_d + local_d) / 16.0
    base_a, base_d = mid_a / 64.0, mid_d / 16.0
    key = jnp.sqrt(key_a * key_a + key_d * key_d)
    base = jnp.sqrt(jnp.zeros_like(key) + (base_a * base_a + base_d * base_d))
    radial = (off_a * (key_a + base_a) + off_d * (key_d + base_d)) / (key + base)
    return TURNS * off_a, TURNS * off_d, TURNS * radial


def fetch(order_hbm, speed_hbm, order_ref, speed_ref, sems):
    copies = [
        pltpu.make_async_copy(order_hbm, order_ref, sems.at[0]),
        pltpu.make_async_copy(speed_hbm, speed_ref, sems.at[1]),
    ]
    for copy in copies:
        copy.start()
    for copy in copies:
        copy.wait()


def wide_code():
    return lax.axis_index("z_hi") * 8 + lax.axis_index("y") * 2 + lax.axis_index("core")


def narrow_place():
    return lax.axis_index("z_lo") * 4 + lax.axis_index("x")


def pull_kernel(
    order_hbm, speed_hbm, spread_ref, x_hbm, o_hbm, order_ref, speed_ref, place_ref, x_ref, o_ref, turned, sems, in_sems, out_sems
):
    arrivals = [pltpu.make_async_copy(x_hbm.at[s], x_ref.at[s], in_sems.at[s]) for s in range(8)]
    for arrival in arrivals:
        arrival.start()
    fetch(order_hbm, speed_hbm, order_ref, speed_ref, sems)
    for j in range(64):
        place_ref[order_ref[j]] = j % 8 * 8 + j // 8
    code = wide_code()
    bits = [(code >> k & 1).astype(jnp.float32) for k in range(4)]
    lane = iota(1)
    node_a, node_d = node_at(iota(0)), node_at(lane % 8)
    center_d = (lane // 8 % 8).astype(jnp.float32) / 8.0 + 0.0625
    center_a, speed = [], []
    for high in range(4):
        center_a.append((lane // 64 + 2 * high).astype(jnp.float32) / 8.0 + 0.0625)
        value = jnp.zeros((8, 128), jnp.float32)
        for low in range(16):
            value = jnp.where(lane // 8 == low, speed_ref[2 * high + low // 8, low % 8], value)
        speed.append(value)
    departures = []
    flat = o_ref.reshape(512, 2, 8, 128)
    for s in range(8):
        super_index = narrow_place() * 8 + s
        table = tables(node_a, node_d, super_index, 2.0 * bits[1] + bits[3], 2.0 * bits[0] + bits[2], 1.0)
        turns = [center_a[h] * table[0] + (center_d * table[1] + speed[h] * table[2]) for h in range(4)]
        cosine, sine = unit(jnp.concatenate(turns, axis=0))
        high, low = split(jnp.concatenate([cosine, sine], axis=0))
        turned[s] = jnp.dot(jnp.concatenate([high, low], axis=1), spread_ref[...], preferred_element_type=jnp.float32)
        arrivals[s].wait()
        for box in range(64):
            place = place_ref[box] + 64 * s
            at, lanes = 8 * (box // 16), 128 * (box % 16)
            cosine = turned[s, at : at + 8, lanes : lanes + 128]
            sine = turned[s, 32 + at : 40 + at, lanes : lanes + 128]
            real, imag = x_ref[s, box, 0], x_ref[s, box, 1]
            flat[place, 0] = real * cosine + imag * sine
            flat[place, 1] = imag * cosine - real * sine
        departure = pltpu.make_async_copy(o_ref.at[s], o_hbm.at[:, s], out_sems.at[s])
        departure.start()
        departures.append(departure)
    for departure in departures:
        departure.wait()


def split(value):
    high = value.astype(jnp.bfloat16)
    return high, (value - high.astype(jnp.float32)).astype(jnp.bfloat16)


def merge_kernel(
    tiles, order_hbm, speed_hbm, across_ref, high_ref, low_ref, x_ref, o_ref, order_ref, speed_ref, rows_h, rows_l, sems
):
    @pl.when(pl.program_id(0) == 0)
    def _():
        fetch(order_hbm, speed_hbm, order_ref, speed_ref, sems)

    code = wide_code()
    across = across_ref[...]
    pairs = [(tile, s) for tile in range(tiles) for s in range(4)]
    for g2 in range(2):
        for g0 in range(2):
            columns = []
            for tile, s in pairs:
                parts = [
                    x_ref[8 * g3 + 4 * g2 + 2 * g1 + g0, s, tile].reshape(16, 128) for g3 in range(2) for g1 in range(2)
                ]
                columns.append(jnp.concatenate(parts, axis=0))
            high, low = split(jnp.concatenate(columns, axis=1))
            moved = jnp.dot(across, jnp.concatenate([high, low, high], axis=0), preferred_element_type=jnp.float32)
            high, low = split(moved)
            lane = 128 * (2 * g2 + g0)
            for p in range(len(pairs)):
                rows_h[64 * p : 64 * p + 64, lane : lane + 128] = high[:, 128 * p : 128 * p + 128]
                rows_l[64 * p : 64 * p + 64, lane : lane + 128] = low[:, 128 * p : 128 * p + 128]
    table = [
        tables(node_at(iota(0)), node_at(iota(1) // 16), narrow_place() * 8 + code % 2 * 4 + s, 0.0, 0.0, 4.0)
        for s in range(4)
    ]
    units = []
    for tile, s in pairs:
        box = order_ref[(pl.program_id(0) * tiles + tile) * 8 + code // 2]
        center_a = (box // 8).astype(jnp.float32) / 8.0 + 0.0625
        center_d = (box % 8).astype(jnp.float32) / 8.0 + 0.0625
        speed = speed_ref[box // 8, box % 8]
        units.append(unit(center_a * table[s][0] + (center_d * table[s][1] + speed * table[s][2])))
    for t0 in range(2):
        wh, wl = high_ref[:, 256 * t0 : 256 * t0 + 256], low_ref[:, 256 * t0 : 256 * t0 + 256]
        total = jnp.dot(rows_h[...], wh, preferred_element_type=jnp.float32)
        total += jnp.dot(rows_l[...], wh, preferred_element_type=jnp.float32)
        total += jnp.dot(rows_h[...], wl, preferred_element_type=jnp.float32)
        for p, (tile, s) in enumerate(pairs):
            cosine, sine = units[p]
            for t3 in range(2):
                for t1 in range(2):
                    at = 64 * p + 16 * t3 + 8 * t1
                    by_re, by_im = total[at : at + 8], total[at + 32 : at + 40]
                    real_re, real_im = by_re[:, :128], by_re[:, 128:]
                    imag_re, imag_im = by_im[:, :128], by_im[:, 128:]
                    for t2, real, imag in (
                        (0, real_re - imag_im, imag_re + real_im),
                        (1, real_re + imag_im, imag_re - real_im),
                    ):
                        low = t0 if t2 == 0 else 1 - t0
                        o_ref[4 * t3 + 2 * t2 + t1, tile, low, s, 0] = real * cosine - imag * sine
                        o_ref[4 * t3 + 2 * t2 + t1, tile, low, s, 1] = real * sine + imag * cosine


ANY = pl.BlockSpec(memory_space=pl.ANY)
LOOKUP = [pltpu.SMEM((64,), jnp.int32), pltpu.SMEM((8, 8), jnp.float32)]


def whole(shape):
    return pl.BlockSpec(shape, lambda i: (0,) * len(shape))


def pull(order, speed, x):
    return pl.pallas_call(
        pull_kernel,
        out_shape=jax.ShapeDtypeStruct((8, 8, 8, 2, 8, 128), jnp.float32),
        in_specs=[ANY, ANY, pl.BlockSpec(memory_space=pltpu.VMEM), ANY],
        out_specs=ANY,
        scratch_shapes=LOOKUP
        + [
            pltpu.SMEM((64,), jnp.int32),
            pltpu.VMEM((8, 64, 2, 8, 128), jnp.float32),
            pltpu.VMEM((8, 8, 8, 2, 8, 128), jnp.float32),
            pltpu.VMEM((8, 64, 2048), jnp.float32),
            pltpu.SemaphoreType.DMA((2,)),
            pltpu.SemaphoreType.DMA((8,)),
            pltpu.SemaphoreType.DMA((8,)),
        ],
        compiler_params=pltpu.CompilerParams(vmem_limit_bytes=60 * 2**20),
    )(order, speed, spread_matrix(), x)


def merge(order, speed, x, tiles=2):
    high, low = down_matrix()
    return pl.pallas_call(
        lambda *refs: merge_kernel(tiles, *refs),
        grid=(8 // tiles,),
        out_shape=jax.ShapeDtypeStruct((8, 8, 2, 4, 2, 8, 128), jnp.float32),
        in_specs=[
            ANY,
            ANY,
            whole((64, 192)),
            whole((512, 512)),
            whole((512, 512)),
            pl.BlockSpec((16, 4, tiles, 2, 8, 128), lambda i: (0, 0, i, 0, 0, 0)),
        ],
        out_specs=pl.BlockSpec((8, tiles, 2, 4, 2, 8, 128), lambda i: (0, i, 0, 0, 0, 0, 0)),
        scratch_shapes=LOOKUP
        + [pltpu.VMEM((256 * tiles, 512), jnp.bfloat16)] * 2
        + [pltpu.SemaphoreType.DMA((2,))],
        compiler_params=pltpu.CompilerParams(vmem_limit_bytes=48 * 2**20),
    )(order, speed, across_matrix(), high, low, x)


def local(weights_in, medium_speed, target_order):
    turned = pull(target_order, medium_speed, weights_in[0])
    gathered = lax.all_to_all(turned.reshape(16, 4, 8, 2, 8, 128), WIDE, 0, 0, tiled=True)
    merged = merge(target_order, medium_speed, gathered)
    chunks = merged.reshape(128, 4, 2, 8, 128)
    spread = lax.all_to_all(chunks, ("z_hi", "y", "z_lo", "x", "core"), 0, 0, tiled=True)
    return spread.reshape(1, 8, 64, 2, 8, 128)


def solution(mesh):
    fine = Mesh(mesh.devices.reshape(FINE_SIZES), FINE)
    split_over = P(WIDE, NARROW, None, None, None, None)
    return jax.shard_map(local, mesh=fine, in_specs=(split_over, P(), P()), out_specs=split_over, check_vma=False)
```

time: 140 us -> 134 us (0.957)
  Pallas kernels: 18.6 us -> 13.4 us
    pallas_call x2, Pallas kernels: 18.6 us -> 13.4 us  [the longest x1 7.61 us: merge(): pl.pallas_call(lambda *refs: merge_kernel(tiles, *refs), grid=(8 // tiles...]
    reshape x1 -> x0, local copies, waits for them, and re-layouts: 2.63 us -> none  [local(): spread = spread.reshape(8, 2, 8, 4, 2, 8, 128)]
    unnamed x10 -> x11, local copies, waits for them, and re-layouts: 0.03 us -> 2.05 us
where the time goes in v3:
time: 134 us
  blocking collectives  118 us (88%)
  Pallas kernels  13.4 us (10%)
  local copies, waits for them, and re-layouts  2.05 us (2%)
    all_to_all x1, blocking collectives, local(): lax.all_to_all(turned.reshape(16, 4, 8, 2, 8, 128), WIDE, 0, 0, tiled=True)  60.3 us
    all_to_all x1, blocking collectives, local(): lax.all_to_all(chunks, ('z_hi', 'y', 'z_lo', 'x', 'core'), 0, 0, tiled=True)  58.1 us
    pallas_call x1, Pallas kernels, merge(): pl.pallas_call(lambda *refs: merge_kernel(tiles, *refs), grid=(8 // tiles...  7.61 us
    pallas_call x1, Pallas kernels, pull(): pl.pallas_call(pull_kernel, out_shape=jax.ShapeDtypeStruct((8, 8, 8, 2, 8...  5.82 us

profile of v3, /device:TPU:1, one launch (start us, length us, event | category | flops | bytes accessed | tf_op | source)
XLA Modules:
  0.0 133.9 jit_solution(5277659335236990180)
XLA Ops:
  0.0 5.8 %shard_map.73 = f32[8,8,8,2,8,128]{5,4,3,2,1,0:T(8,128)} custom-call(s32[64]{0:T(128)} %refs_0_.1, f32[8,8]{1,0:T(8,128)} %refs_1_.1, bf16[256,2048]{1,0:T(8,128)(2,1)} %constant.8.clone.spread_ref, f32[8,64,2,8,128]{4,3,2,1,0:T(8,128)} %bitcast.7), custom_call_target="tpu_custom_call" | custom-call | tf_op jit(solution)/shard_map/pallas_call | solution.py:255
  5.8 0.0 copy-start
  5.8 0.0 copy-start.1
  5.9 0.0 copy-start.2
  5.9 0.0 copy-start.3
  5.9 0.0 copy-start.4
  5.9 60.3 %all_to_all.10.refs_5_ = f32[16,4,8,2,8,128]{5,4,3,2,1,0:T(8,128)} all-to-all(f32[16,4,8,2,8,128]{5,4,3,2,1,0:T(8,128)} %bitcast.5), channel_id=1, replica_groups=mesh['z_hi'=2,'y'=4,'core'=2,'z_lo'=2,'x'=4] {'z_hi','y','core'}, dimensions={0} | all-to-all | bytes 8388608 | tf_op jit(solution)/shard_map/all_to_all | solution.py:298
  66.1 0.0 copy-done
  66.2 0.0 copy-done.1
  66.2 0.0 copy-done.2
  66.2 0.0 copy-done.3
  66.2 0.0 copy-done.4
  66.2 7.6 %shard_map.74 = f32[8,8,2,4,2,8,128]{6,5,4,3,2,1,0:T(8,128)S(1)} custom-call(s32[64]{0:T(128)S(1)} %copy-done.4, f32[8,8]{1,0:T(8,128)S(1)} %copy-done.3, bf16[64,192]{1,0:T(8,128)(2,1)S(1)} %copy-done.2, bf16[512,512]{1,0:T(8,128)(2,1)S(1)} %copy-done.1, bf16[512,512]{1,0:T(8,128)(2,1)S(1)} %copy-done, f32[16,4,8,2,8,128]{5,4,3,2,1,0:T(8,128)} %all_to_all.10.refs_5_), custom_call_target="tpu_custom_call" | custom-call | tf_op jit(solution)/shard_map/pallas_call | solution.py:276
  73.8 58.1 %all_to_all.11 = f32[128,4,2,8,128]{4,3,2,1,0:T(8,128)S(1)} all-to-all(f32[128,4,2,8,128]{4,3,2,1,0:T(8,128)S(1)} %bitcast.4), channel_id=1, replica_groups=mesh['z_hi'=2,'y'=4,'core'=2,'z_lo'=2,'x'=4] {'z_hi','y','z_lo','x','core'}, dimensions={0} | all-to-all | bytes 8388608 | tf_op jit(solution)/shard_map/all_to_all | solution.py:301
  131.9 2.0 %copy.9 = f32[1,8,64,2,8,128]{5,4,3,2,1,0:T(8,128)} copy(f32[1,8,64,2,8,128]{5,4,3,2,1,0:T(8,128)S(1)} %bitcast.6) | data formatting | bytes 8388608
Async XLA Ops:
  5.8 60.3 %copy-start = (bf16[512,512]{1,0:T(8,128)(2,1)S(1)}, bf16[512,512]{1,0:T(8,128)(2,1)}, u32[]{:S(2)}) copy-start(bf16[512,512]{1,0:T(8,128)(2,1)} %constant.11.clone.refs_4_) | copy-start | bytes 1572868
  5.8 60.3 %copy-start.1 = (bf16[512,512]{1,0:T(8,128)(2,1)S(1)}, bf16[512,512]{1,0:T(8,128)(2,1)}, u32[]{:S(2)}) copy-start(bf16[512,512]{1,0:T(8,128)(2,1)} %constant.10.clone.refs_3_) | copy-start | bytes 1572868
  5.9 60.3 %copy-start.2 = (bf16[64,192]{1,0:T(8,128)(2,1)S(1)}, bf16[64,192]{1,0:T(8,128)(2,1)}, u32[]{:S(2)}) copy-start(bf16[64,192]{1,0:T(8,128)(2,1)} %constant.9.clone.refs_2_) | copy-start | bytes 73732
  5.9 60.3 %copy-start.3 = (f32[8,8]{1,0:T(8,128)S(1)}, f32[8,8]{1,0:T(8,128)}, u32[]{:S(2)}) copy-start(f32[8,8]{1,0:T(8,128)} %refs_1_.1) | copy-start | bytes 772
  5.9 60.3 %copy-start.4 = (s32[64]{0:T(128)S(1)}, s32[64]{0:T(128)}, u32[]{:S(2)}) copy-start(s32[64]{0:T(128)} %refs_0_.1) | copy-start | bytes 772

commit v4 on v3

--- a/solution.py
+++ b/solution.py
@@ -72,8 +72,7 @@
     one = np.zeros((16, 8, 16, 8, 16))
     for box in range(16):
         one[box, np.arange(8), box, np.arange(8)] = 1.0
-    one = one.reshape(128, 2048)
-    return np.concatenate([one, one]).astype(jnp.bfloat16)
+    return one.reshape(128, 2048).astype(jnp.bfloat16)
 
 
 def horner(coefficients, x):
@@ -115,15 +114,11 @@
     return TURNS * off_a, TURNS * off_d, TURNS * radial
 
 
-def fetch(order_hbm, speed_hbm, order_ref, speed_ref, sems):
-    copies = [
-        pltpu.make_async_copy(order_hbm, order_ref, sems.at[0]),
-        pltpu.make_async_copy(speed_hbm, speed_ref, sems.at[1]),
-    ]
+def fetch(sources, targets, sems):
+    copies = [pltpu.make_async_copy(*pair, sems.at[k]) for k, pair in enumerate(zip(sources, targets))]
     for copy in copies:
         copy.start()
-    for copy in copies:
-        copy.wait()
+    return copies
 
 
 def wide_code():
@@ -135,41 +130,70 @@
 
 
 def pull_kernel(
-    order_hbm, speed_hbm, spread_ref, x_hbm, o_hbm, order_ref, speed_ref, place_ref, x_ref, o_ref, turned, sems, in_sems, out_sems
+    order_hbm,
+    speed_hbm,
+    spread_hbm,
+    x_hbm,
+    o_hbm,
+    order_ref,
+    speed_ref,
+    place_ref,
+    spread_ref,
+    x_ref,
+    o_ref,
+    turned,
+    sems,
+    in_sems,
+    out_sems,
 ):
+    lookups = fetch((order_hbm, speed_hbm, spread_hbm), (order_ref, speed_ref, spread_ref), sems)
     arrivals = [pltpu.make_async_copy(x_hbm.at[s], x_ref.at[s], in_sems.at[s]) for s in range(8)]
     for arrival in arrivals:
         arrival.start()
-    fetch(order_hbm, speed_hbm, order_ref, speed_ref, sems)
-    for j in range(64):
-        place_ref[order_ref[j]] = j % 8 * 8 + j // 8
     code = wide_code()
     bits = [(code >> k & 1).astype(jnp.float32) for k in range(4)]
     lane = iota(1)
     node_a, node_d = node_at(iota(0)), node_at(lane % 8)
+    center_a = [(lane // 64 + 2 * high).astype(jnp.float32) / 8.0 + 0.0625 for high in range(4)]
     center_d = (lane // 8 % 8).astype(jnp.float32) / 8.0 + 0.0625
-    center_a, speed = [], []
+    plane, radial = [], []
+    for s in range(8):
+        super_index = narrow_place() * 8 + s
+        table = tables(node_a, node_d, super_index, 2.0 * bits[1] + bits[3], 2.0 * bits[0] + bits[2], 1.0)
+        plane.append([center_a[high] * table[0] + center_d * table[1] for high in range(4)])
+        radial.append(table[2])
+    lookups[1].wait()
+    speed = []
     for high in range(4):
-        center_a.append((lane // 64 + 2 * high).astype(jnp.float32) / 8.0 + 0.0625)
         value = jnp.zeros((8, 128), jnp.float32)
         for low in range(16):
             value = jnp.where(lane // 8 == low, speed_ref[2 * high + low // 8, low % 8], value)
         speed.append(value)
+    lookups[0].wait()
+    for j in range(64):
+        place_ref[order_ref[j]] = j % 8 * 8 + j // 8
+    lookups[2].wait()
+
+    def spread(group):
+        both_supers = (2 * group, 2 * group + 1)
+        angles = [plane[s][high] + speed[high] * radial[s] for s in both_supers for high in range(4)]
+        cosine, sine = unit(jnp.concatenate(angles, axis=0))
+        high, low = split(jnp.concatenate([cosine[:32], sine[:32], cosine[32:], sine[32:]], axis=0))
+        both = jnp.dot(jnp.concatenate([high, low], axis=0), spread_ref[...], preferred_element_type=jnp.float32)
+        turned[128 * group : 128 * group + 128] = both[:128] + both[128:]
+
+    spread(0)
     departures = []
     flat = o_ref.reshape(512, 2, 8, 128)
     for s in range(8):
-        super_index = narrow_place() * 8 + s
-        table = tables(node_a, node_d, super_index, 2.0 * bits[1] + bits[3], 2.0 * bits[0] + bits[2], 1.0)
-        turns = [center_a[h] * table[0] + (center_d * table[1] + speed[h] * table[2]) for h in range(4)]
-        cosine, sine = unit(jnp.concatenate(turns, axis=0))
-        high, low = split(jnp.concatenate([cosine, sine], axis=0))
-        turned[s] = jnp.dot(jnp.concatenate([high, low], axis=1), spread_ref[...], preferred_element_type=jnp.float32)
         arrivals[s].wait()
+        if s % 2 == 1 and s < 7:
+            spread(s // 2 + 1)
         for box in range(64):
             place = place_ref[box] + 64 * s
-            at, lanes = 8 * (box // 16), 128 * (box % 16)
-            cosine = turned[s, at : at + 8, lanes : lanes + 128]
-            sine = turned[s, 32 + at : 40 + at, lanes : lanes + 128]
+            at, lanes = 64 * s + 8 * (box // 16), 128 * (box % 16)
+            cosine = turned[at : at + 8, lanes : lanes + 128]
+            sine = turned[32 + at : 40 + at, lanes : lanes + 128]
             real, imag = x_ref[s, box, 0], x_ref[s, box, 1]
             flat[place, 0] = real * cosine + imag * sine
             flat[place, 1] = imag * cosine - real * sine
@@ -186,15 +210,17 @@
 
 
 def merge_kernel(
-    tiles, order_hbm, speed_hbm, across_ref, high_ref, low_ref, x_ref, o_ref, order_ref, speed_ref, rows_h, rows_l, sems
+    tiles, order_hbm, speed_hbm, across_ref, high_ref, low_ref, x_ref, o_ref, order_ref, speed_ref, rows, sems
 ):
     @pl.when(pl.program_id(0) == 0)
     def _():
-        fetch(order_hbm, speed_hbm, order_ref, speed_ref, sems)
+        for copy in fetch((order_hbm, speed_hbm), (order_ref, speed_ref), sems):
+            copy.wait()
 
     code = wide_code()
     across = across_ref[...]
     pairs = [(tile, s) for tile in range(tiles) for s in range(4)]
+    size = 64 * len(pairs)
     for g2 in range(2):
         for g0 in range(2):
             columns = []
@@ -208,8 +234,8 @@
             high, low = split(moved)
             lane = 128 * (2 * g2 + g0)
             for p in range(len(pairs)):
-                rows_h[64 * p : 64 * p + 64, lane : lane + 128] = high[:, 128 * p : 128 * p + 128]
-                rows_l[64 * p : 64 * p + 64, lane : lane + 128] = low[:, 128 * p : 128 * p + 128]
+                rows[64 * p : 64 * p + 64, lane : lane + 128] = high[:, 128 * p : 128 * p + 128]
+                rows[size + 64 * p : size + 64 * p + 64, lane : lane + 128] = low[:, 128 * p : 128 * p + 128]
     table = [
         tables(node_at(iota(0)), node_at(iota(1) // 16), narrow_place() * 8 + code % 2 * 4 + s, 0.0, 0.0, 4.0)
         for s in range(4)
@@ -223,9 +249,8 @@
         units.append(unit(center_a * table[s][0] + (center_d * table[s][1] + speed * table[s][2])))
     for t0 in range(2):
         wh, wl = high_ref[:, 256 * t0 : 256 * t0 + 256], low_ref[:, 256 * t0 : 256 * t0 + 256]
-        total = jnp.dot(rows_h[...], wh, preferred_element_type=jnp.float32)
-        total += jnp.dot(rows_l[...], wh, preferred_element_type=jnp.float32)
-        total += jnp.dot(rows_h[...], wl, preferred_element_type=jnp.float32)
+        both = jnp.dot(rows[...], wh, preferred_element_type=jnp.float32)
+        total = both[:size] + both[size:] + jnp.dot(rows[:size], wl, preferred_element_type=jnp.float32)
         for p, (tile, s) in enumerate(pairs):
             cosine, sine = units[p]
             for t3 in range(2):
@@ -255,15 +280,16 @@
     return pl.pallas_call(
         pull_kernel,
         out_shape=jax.ShapeDtypeStruct((8, 8, 8, 2, 8, 128), jnp.float32),
-        in_specs=[ANY, ANY, pl.BlockSpec(memory_space=pltpu.VMEM), ANY],
+        in_specs=[ANY, ANY, ANY, ANY],
         out_specs=ANY,
         scratch_shapes=LOOKUP
         + [
             pltpu.SMEM((64,), jnp.int32),
+            pltpu.VMEM((128, 2048), jnp.bfloat16),
             pltpu.VMEM((8, 64, 2, 8, 128), jnp.float32),
             pltpu.VMEM((8, 8, 8, 2, 8, 128), jnp.float32),
-            pltpu.VMEM((8, 64, 2048), jnp.float32),
-            pltpu.SemaphoreType.DMA((2,)),
+            pltpu.VMEM((512, 2048), jnp.float32),
+            pltpu.SemaphoreType.DMA((3,)),
             pltpu.SemaphoreType.DMA((8,)),
             pltpu.SemaphoreType.DMA((8,)),
         ],
@@ -287,9 +313,9 @@
         ],
         out_specs=pl.BlockSpec((8, tiles, 2, 4, 2, 8, 128), lambda i: (0, i, 0, 0, 0, 0, 0)),
         scratch_shapes=LOOKUP
-        + [pltpu.VMEM((256 * tiles, 512), jnp.bfloat16)] * 2
+        + [pltpu.VMEM((512 * tiles, 512), jnp.bfloat16)]
         + [pltpu.SemaphoreType.DMA((2,))],
-        compiler_params=pltpu.CompilerParams(vmem_limit_bytes=48 * 2**20),
+        compiler_params=pltpu.CompilerParams(vmem_limit_bytes=32 * 2**20),
     )(order, speed, across_matrix(), high, low, x)
 
 

time: 134 us -> 133 us (level)
  no operation moved by 1% of the time
where the time goes in v4:
time: 133 us; the launch traced here: 132 us
  blocking collectives  118 us (89%)
  Pallas kernels  12.1 us (9%)
  local copies, waits for them, and re-layouts  2.05 us (2%)
    all_to_all x1, blocking collectives, local(): lax.all_to_all(turned.reshape(16, 4, 8, 2, 8, 128), WIDE, 0, 0, tiled=True)  60.1 us
    all_to_all x1, blocking collectives, local(): lax.all_to_all(chunks, ('z_hi', 'y', 'z_lo', 'x', 'core'), 0, 0, tiled=True)  58.1 us
    pallas_call x1, Pallas kernels, merge(): pl.pallas_call(lambda *refs: merge_kernel(tiles, *refs), grid=(8 // tiles...  6.77 us
    pallas_call x1, Pallas kernels, pull(): pl.pallas_call(pull_kernel, out_shape=jax.ShapeDtypeStruct((8, 8, 8, 2, 8...  5.29 us

profile of v4, /device:TPU:1, one launch (start us, length us, event | category | flops | bytes accessed | tf_op | source)
XLA Modules:
  0.0 132.4 jit_solution(6327197873703920747)
XLA Ops:
  0.0 5.3 %shard_map.73 = f32[8,8,8,2,8,128]{5,4,3,2,1,0:T(8,128)} custom-call(s32[64]{0:T(128)} %refs_0_.1, f32[8,8]{1,0:T(8,128)} %refs_1_.1, bf16[128,2048]{1,0:T(8,128)(2,1)} %constant.8.clone.spread_hbm, f32[8,64,2,8,128]{4,3,2,1,0:T(8,128)} %bitcast.7), custom_call_target="tpu_custom_call" | custom-call | tf_op jit(solution)/shard_map/pallas_call | solution.py:280
  5.3 0.0 copy-start
  5.3 0.0 copy-start.1
  5.3 0.0 copy-start.2
  5.3 0.0 copy-start.3
  5.3 0.0 copy-start.4
  5.4 60.1 %all_to_all.10.refs_5_ = f32[16,4,8,2,8,128]{5,4,3,2,1,0:T(8,128)S(1)} all-to-all(f32[16,4,8,2,8,128]{5,4,3,2,1,0:T(8,128)} %bitcast.5), channel_id=1, replica_groups=mesh['z_hi'=2,'y'=4,'core'=2,'z_lo'=2,'x'=4] {'z_hi','y','core'}, dimensions={0} | all-to-all | bytes 8388608 | tf_op jit(solution)/shard_map/all_to_all | solution.py:324
  65.5 0.0 copy-done
  65.5 0.0 copy-done.1
  65.5 0.0 copy-done.2
  65.5 0.0 copy-done.3
  65.5 0.0 copy-done.4
  65.5 6.8 %shard_map.74 = f32[8,8,2,4,2,8,128]{6,5,4,3,2,1,0:T(8,128)S(1)} custom-call(s32[64]{0:T(128)S(1)} %copy-done.4, f32[8,8]{1,0:T(8,128)S(1)} %copy-done.3, bf16[64,192]{1,0:T(8,128)(2,1)S(1)} %copy-done.2, bf16[512,512]{1,0:T(8,128)(2,1)S(1)} %copy-done.1, bf16[512,512]{1,0:T(8,128)(2,1)S(1)} %copy-done, f32[16,4,8,2,8,128]{5,4,3,2,1,0:T(8,128)S(1)} %all_to_all.10.refs_5_), custom_call_target="tpu_custom_call" | custom-call | tf_op jit(solution)/shard_map/pallas_call | solution.py:302
  72.3 58.1 %all_to_all.11 = f32[128,4,2,8,128]{4,3,2,1,0:T(8,128)S(1)} all-to-all(f32[128,4,2,8,128]{4,3,2,1,0:T(8,128)S(1)} %bitcast.4), channel_id=1, replica_groups=mesh['z_hi'=2,'y'=4,'core'=2,'z_lo'=2,'x'=4] {'z_hi','y','z_lo','x','core'}, dimensions={0} | all-to-all | bytes 8388608 | tf_op jit(solution)/shard_map/all_to_all | solution.py:327
  130.4 2.0 %copy.9 = f32[1,8,64,2,8,128]{5,4,3,2,1,0:T(8,128)} copy(f32[1,8,64,2,8,128]{5,4,3,2,1,0:T(8,128)S(1)} %bitcast.6) | data formatting | bytes 8388608
Async XLA Ops:
  5.3 60.2 %copy-start = (bf16[512,512]{1,0:T(8,128)(2,1)S(1)}, bf16[512,512]{1,0:T(8,128)(2,1)}, u32[]{:S(2)}) copy-start(bf16[512,512]{1,0:T(8,128)(2,1)} %constant.11.clone.refs_4_) | copy-start | bytes 1572868
  5.3 60.2 %copy-start.1 = (bf16[512,512]{1,0:T(8,128)(2,1)S(1)}, bf16[512,512]{1,0:T(8,128)(2,1)}, u32[]{:S(2)}) copy-start(bf16[512,512]{1,0:T(8,128)(2,1)} %constant.10.clone.refs_3_) | copy-start | bytes 1572868
  5.3 60.2 %copy-start.2 = (bf16[64,192]{1,0:T(8,128)(2,1)S(1)}, bf16[64,192]{1,0:T(8,128)(2,1)}, u32[]{:S(2)}) copy-start(bf16[64,192]{1,0:T(8,128)(2,1)} %constant.9.clone.refs_2_) | copy-start | bytes 73732
  5.3 60.2 %copy-start.3 = (f32[8,8]{1,0:T(8,128)S(1)}, f32[8,8]{1,0:T(8,128)}, u32[]{:S(2)}) copy-start(f32[8,8]{1,0:T(8,128)} %refs_1_.1) | copy-start | bytes 772
  5.3 60.2 %copy-start.4 = (s32[64]{0:T(128)S(1)}, s32[64]{0:T(128)}, u32[]{:S(2)}) copy-start(s32[64]{0:T(128)} %refs_0_.1) | copy-start | bytes 772

commit v5 on v4

--- a/solution.py
+++ b/solution.py
@@ -66,13 +66,6 @@
     move = np.transpose(dimension_operator(16), (3, 4, 5, 0, 1, 2))[:, :, :, 0]
     real = np.stack([move.real, move.imag], axis=4)
     return halves(np.kron(real.reshape(32, 32), np.eye(16)))
-
-
-def spread_matrix():
-    one = np.zeros((16, 8, 16, 8, 16))
-    for box in range(16):
-        one[box, np.arange(8), box, np.arange(8)] = 1.0
-    return one.reshape(128, 2048).astype(jnp.bfloat16)
 
 
 def horner(coefficients, x):
@@ -114,13 +107,6 @@
     return TURNS * off_a, TURNS * off_d, TURNS * radial
 
 
-def fetch(sources, targets, sems):
-    copies = [pltpu.make_async_copy(*pair, sems.at[k]) for k, pair in enumerate(zip(sources, targets))]
-    for copy in copies:
-        copy.start()
-    return copies
-
-
 def wide_code():
     return lax.axis_index("z_hi") * 8 + lax.axis_index("y") * 2 + lax.axis_index("core")
 
@@ -130,23 +116,10 @@
 
 
 def pull_kernel(
-    order_hbm,
-    speed_hbm,
-    spread_hbm,
-    x_hbm,
-    o_hbm,
-    order_ref,
-    speed_ref,
-    place_ref,
-    spread_ref,
-    x_ref,
-    o_ref,
-    turned,
-    sems,
-    in_sems,
-    out_sems,
+    lookup_hbm, x_hbm, o_hbm, lookup_ref, place_ref, spread_ref, x_ref, o_ref, turned, sem, in_sems, out_sems
 ):
-    lookups = fetch((order_hbm, speed_hbm, spread_hbm), (order_ref, speed_ref, spread_ref), sems)
+    lookup = pltpu.make_async_copy(lookup_hbm, lookup_ref, sem)
+    lookup.start()
     arrivals = [pltpu.make_async_copy(x_hbm.at[s], x_ref.at[s], in_sems.at[s]) for s in range(8)]
     for arrival in arrivals:
         arrival.start()
@@ -162,17 +135,21 @@
         table = tables(node_a, node_d, super_index, 2.0 * bits[1] + bits[3], 2.0 * bits[0] + bits[2], 1.0)
         plane.append([center_a[high] * table[0] + center_d * table[1] for high in range(4)])
         radial.append(table[2])
-    lookups[1].wait()
+    spread_ref[...] = jnp.zeros_like(spread_ref)
+    row = lax.broadcasted_iota(jnp.int32, (16, 128), 0)
+    point = lax.broadcasted_iota(jnp.int32, (16, 128), 1) // 16
+    for box in range(16):
+        same = jnp.where(row == box % 2 * 8 + point, 1.0, 0.0).astype(jnp.bfloat16)
+        spread_ref[box // 2 * 16 : box // 2 * 16 + 16, 128 * box : 128 * box + 128] = same
+    lookup.wait()
     speed = []
     for high in range(4):
         value = jnp.zeros((8, 128), jnp.float32)
         for low in range(16):
-            value = jnp.where(lane // 8 == low, speed_ref[2 * high + low // 8, low % 8], value)
+            value = jnp.where(lane // 8 == low, lookup_ref[2 * high + low // 8, low % 8], value)
         speed.append(value)
-    lookups[0].wait()
     for j in range(64):
-        place_ref[order_ref[j]] = j % 8 * 8 + j // 8
-    lookups[2].wait()
+        place_ref[lookup_ref[8, j].astype(jnp.int32)] = j % 8 * 8 + j // 8
 
     def spread(group):
         both_supers = (2 * group, 2 * group + 1)
@@ -210,12 +187,13 @@
 
 
 def merge_kernel(
-    tiles, order_hbm, speed_hbm, across_ref, high_ref, low_ref, x_ref, o_ref, order_ref, speed_ref, rows, sems
+    tiles, lookup_hbm, across_ref, high_ref, low_ref, x_ref, o_ref, lookup_ref, rows, sem
 ):
     @pl.when(pl.program_id(0) == 0)
     def _():
-        for copy in fetch((order_hbm, speed_hbm), (order_ref, speed_ref), sems):
-            copy.wait()
+        lookup = pltpu.make_async_copy(lookup_hbm, lookup_ref, sem)
+        lookup.start()
+        lookup.wait()
 
     code = wide_code()
     across = across_ref[...]
@@ -242,10 +220,10 @@
     ]
     units = []
     for tile, s in pairs:
-        box = order_ref[(pl.program_id(0) * tiles + tile) * 8 + code // 2]
+        box = lookup_ref[8, (pl.program_id(0) * tiles + tile) * 8 + code // 2].astype(jnp.int32)
         center_a = (box // 8).astype(jnp.float32) / 8.0 + 0.0625
         center_d = (box % 8).astype(jnp.float32) / 8.0 + 0.0625
-        speed = speed_ref[box // 8, box % 8]
+        speed = lookup_ref[box // 8, box % 8]
         units.append(unit(center_a * table[s][0] + (center_d * table[s][1] + speed * table[s][2])))
     for t0 in range(2):
         wh, wl = high_ref[:, 256 * t0 : 256 * t0 + 256], low_ref[:, 256 * t0 : 256 * t0 + 256]
@@ -269,35 +247,35 @@
 
 
 ANY = pl.BlockSpec(memory_space=pl.ANY)
-LOOKUP = [pltpu.SMEM((64,), jnp.int32), pltpu.SMEM((8, 8), jnp.float32)]
+LOOKUP = pltpu.SMEM((9, 64), jnp.float32)
 
 
 def whole(shape):
     return pl.BlockSpec(shape, lambda i: (0,) * len(shape))
 
 
-def pull(order, speed, x):
+def pull(lookup, x):
     return pl.pallas_call(
         pull_kernel,
         out_shape=jax.ShapeDtypeStruct((8, 8, 8, 2, 8, 128), jnp.float32),
-        in_specs=[ANY, ANY, ANY, ANY],
+        in_specs=[ANY, ANY],
         out_specs=ANY,
-        scratch_shapes=LOOKUP
-        + [
+        scratch_shapes=[
+            LOOKUP,
             pltpu.SMEM((64,), jnp.int32),
             pltpu.VMEM((128, 2048), jnp.bfloat16),
             pltpu.VMEM((8, 64, 2, 8, 128), jnp.float32),
             pltpu.VMEM((8, 8, 8, 2, 8, 128), jnp.float32),
             pltpu.VMEM((512, 2048), jnp.float32),
-            pltpu.SemaphoreType.DMA((3,)),
+            pltpu.SemaphoreType.DMA,
             pltpu.SemaphoreType.DMA((8,)),
             pltpu.SemaphoreType.DMA((8,)),
         ],
-        compiler_params=pltpu.CompilerParams(vmem_limit_bytes=60 * 2**20),
-    )(order, speed, spread_matrix(), x)
-
-
-def merge(order, speed, x, tiles=2):
+        compiler_params=pltpu.CompilerParams(vmem_limit_bytes=48 * 2**20),
+    )(lookup, x)
+
+
+def merge(lookup, x, tiles=2):
     high, low = down_matrix()
     return pl.pallas_call(
         lambda *refs: merge_kernel(tiles, *refs),
@@ -305,24 +283,23 @@
         out_shape=jax.ShapeDtypeStruct((8, 8, 2, 4, 2, 8, 128), jnp.float32),
         in_specs=[
             ANY,
-            ANY,
             whole((64, 192)),
             whole((512, 512)),
             whole((512, 512)),
             pl.BlockSpec((16, 4, tiles, 2, 8, 128), lambda i: (0, 0, i, 0, 0, 0)),
         ],
         out_specs=pl.BlockSpec((8, tiles, 2, 4, 2, 8, 128), lambda i: (0, i, 0, 0, 0, 0, 0)),
-        scratch_shapes=LOOKUP
-        + [pltpu.VMEM((512 * tiles, 512), jnp.bfloat16)]
-        + [pltpu.SemaphoreType.DMA((2,))],
+        scratch_shapes=[LOOKUP, pltpu.VMEM((512 * tiles, 512), jnp.bfloat16), pltpu.SemaphoreType.DMA],
         compiler_params=pltpu.CompilerParams(vmem_limit_bytes=32 * 2**20),
-    )(order, speed, across_matrix(), high, low, x)
+    )(lookup, across_matrix(), high, low, x)
 
 
 def local(weights_in, medium_speed, target_order):
-    turned = pull(target_order, medium_speed, weights_in[0])
+    speeds = jnp.pad(medium_speed, ((0, 0), (0, 56)))
+    lookup = jnp.concatenate([speeds, target_order.astype(jnp.float32)[None]], axis=0)
+    turned = pull(lookup, weights_in[0])
     gathered = lax.all_to_all(turned.reshape(16, 4, 8, 2, 8, 128), WIDE, 0, 0, tiled=True)
-    merged = merge(target_order, medium_speed, gathered)
+    merged = merge(lookup, gathered)
     chunks = merged.reshape(128, 4, 2, 8, 128)
     spread = lax.all_to_all(chunks, ("z_hi", "y", "z_lo", "x", "core"), 0, 0, tiled=True)
     return spread.reshape(1, 8, 64, 2, 8, 128)

time: 133 us -> 132 us (level)
  Pallas kernels: 12.1 us -> 10.2 us
  other arithmetic: 0 us -> 1.35 us
    pallas_call x1, Pallas kernels: 5.29 us -> 3.38 us  [pull(): pl.pallas_call(pull_kernel, out_shape=jax.ShapeDtypeStruct((8, 8, 8, 2, 8...]
where the time goes in v5:
time: 132 us
  blocking collectives  118 us (89%)
  Pallas kernels  10.2 us (8%)
  local copies, waits for them, and re-layouts  2.03 us (2%)
  other arithmetic  1.35 us (1%)
    all_to_all x1, blocking collectives, local(): lax.all_to_all(turned.reshape(16, 4, 8, 2, 8, 128), WIDE, 0, 0, tiled=True)  59.9 us
    all_to_all x1, blocking collectives, local(): lax.all_to_all(chunks, ('z_hi', 'y', 'z_lo', 'x', 'core'), 0, 0, tiled=True)  58.1 us
    pallas_call x1, Pallas kernels, merge(): pl.pallas_call(lambda *refs: merge_kernel(tiles, *refs), grid=(8 // tiles...  6.8 us
    pallas_call x1, Pallas kernels, pull(): pl.pallas_call(pull_kernel, out_shape=jax.ShapeDtypeStruct((8, 8, 8, 2, 8...  3.38 us

profile of v5, /device:TPU:1, one launch (start us, length us, event | category | flops | bytes accessed | tf_op | source)
XLA Modules:
  0.0 131.6 jit_solution(3525337527455401993)
XLA Ops:
  0.0 0.7 convert_bitcast_fusion
  0.7 0.7 select_maximum_fusion.lookup_hbm.refs_0_
  1.4 3.4 %shard_map.64 = f32[8,8,8,2,8,128]{5,4,3,2,1,0:T(8,128)S(1)} custom-call(f32[9,64]{1,0:T(8,128)S(1)} %select_maximum_fusion.lookup_hbm.refs_0_, f32[8,64,2,8,128]{4,3,2,1,0:T(8,128)} %bitcast.9), custom_call_target="tpu_custom_call" | custom-call | tf_op jit(solution)/shard_map/pallas_call | solution.py:258
  4.7 0.0 copy-start
  4.8 0.0 copy-start.1
  4.8 0.0 copy-start.2
  4.8 59.9 %all_to_all.10.refs_4_ = f32[16,4,8,2,8,128]{5,4,3,2,1,0:T(8,128)S(1)} all-to-all(f32[16,4,8,2,8,128]{5,4,3,2,1,0:T(8,128)S(1)} %bitcast.6), channel_id=1, replica_groups=mesh['z_hi'=2,'y'=4,'core'=2,'z_lo'=2,'x'=4] {'z_hi','y','core'}, dimensions={0} | all-to-all | bytes 8388608 | tf_op jit(solution)/shard_map/all_to_all | solution.py:301
  64.7 0.0 copy-done
  64.7 0.0 copy-done.1
  64.7 0.0 copy-done.2
  64.7 6.8 %shard_map.65 = f32[8,8,2,4,2,8,128]{6,5,4,3,2,1,0:T(8,128)S(1)} custom-call(f32[9,64]{1,0:T(8,128)S(1)} %select_maximum_fusion.lookup_hbm.refs_0_, bf16[64,192]{1,0:T(8,128)(2,1)S(1)} %copy-done.2, bf16[512,512]{1,0:T(8,128)(2,1)S(1)} %copy-done.1, bf16[512,512]{1,0:T(8,128)(2,1)S(1)} %copy-done, f32[16,4,8,2,8,128]{5,4,3,2,1,0:T(8,128)S(1)} %all_to_all.10.refs_4_), custom_call_target="tpu_custom_call" | custom-call | tf_op jit(solution)/shard_map/pallas_call | solution.py:280
  71.5 58.1 %all_to_all.11 = f32[128,4,2,8,128]{4,3,2,1,0:T(8,128)S(1)} all-to-all(f32[128,4,2,8,128]{4,3,2,1,0:T(8,128)S(1)} %bitcast.7), channel_id=1, replica_groups=mesh['z_hi'=2,'y'=4,'core'=2,'z_lo'=2,'x'=4] {'z_hi','y','z_lo','x','core'}, dimensions={0} | all-to-all | bytes 8388608 | tf_op jit(solution)/shard_map/all_to_all | solution.py:304
  129.6 2.0 %copy.8 = f32[1,8,64,2,8,128]{5,4,3,2,1,0:T(8,128)} copy(f32[1,8,64,2,8,128]{5,4,3,2,1,0:T(8,128)S(1)} %bitcast.8) | data formatting | bytes 8388608
Async XLA Ops:
  4.7 60.0 %copy-start = (bf16[512,512]{1,0:T(8,128)(2,1)S(1)}, bf16[512,512]{1,0:T(8,128)(2,1)}, u32[]{:S(2)}) copy-start(bf16[512,512]{1,0:T(8,128)(2,1)} %constant.11.clone.refs_3_) | copy-start | bytes 1572868
  4.8 60.0 %copy-start.1 = (bf16[512,512]{1,0:T(8,128)(2,1)S(1)}, bf16[512,512]{1,0:T(8,128)(2,1)}, u32[]{:S(2)}) copy-start(bf16[512,512]{1,0:T(8,128)(2,1)} %constant.10.clone.refs_2_) | copy-start | bytes 1572868
  4.8 60.0 %copy-start.2 = (bf16[64,192]{1,0:T(8,128)(2,1)S(1)}, bf16[64,192]{1,0:T(8,128)(2,1)}, u32[]{:S(2)}) copy-start(bf16[64,192]{1,0:T(8,128)(2,1)} %constant.9.clone.refs_1_) | copy-start | bytes 73732

commit v6 on v5

--- a/solution.py
+++ b/solution.py
@@ -116,7 +116,21 @@
 
 
 def pull_kernel(
-    lookup_hbm, x_hbm, o_hbm, lookup_ref, place_ref, spread_ref, x_ref, o_ref, turned, sem, in_sems, out_sems
+    lookup_hbm,
+    x_hbm,
+    o_hbm,
+    push_hbm,
+    lookup_ref,
+    place_ref,
+    spread_ref,
+    x_ref,
+    o_ref,
+    push_ref,
+    turned,
+    sem,
+    push_sem,
+    in_sems,
+    out_sems,
 ):
     lookup = pltpu.make_async_copy(lookup_hbm, lookup_ref, sem)
     lookup.start()
@@ -160,6 +174,20 @@
         turned[128 * group : 128 * group + 128] = both[:128] + both[128:]
 
     spread(0)
+    table = [
+        tables(node_a, node_at(lane // 16), narrow_place() * 8 + code % 2 * 4 + s, 0.0, 0.0, 4.0) for s in range(4)
+    ]
+    for tile in range(8):
+        box = lookup_ref[8, tile * 8 + code // 2].astype(jnp.int32)
+        across = (box // 8).astype(jnp.float32) / 8.0 + 0.0625
+        down = (box % 8).astype(jnp.float32) / 8.0 + 0.0625
+        at_box = lookup_ref[box // 8, box % 8]
+        for s in range(4):
+            cosine, sine = unit(across * table[s][0] + (down * table[s][1] + at_box * table[s][2]))
+            push_ref[tile, s, 0] = cosine
+            push_ref[tile, s, 1] = sine
+    push_copy = pltpu.make_async_copy(push_ref, push_hbm, push_sem)
+    push_copy.start()
     departures = []
     flat = o_ref.reshape(512, 2, 8, 128)
     for s in range(8):
@@ -177,6 +205,7 @@
         departure = pltpu.make_async_copy(o_ref.at[s], o_hbm.at[:, s], out_sems.at[s])
         departure.start()
         departures.append(departure)
+    push_copy.wait()
     for departure in departures:
         departure.wait()
 
@@ -187,15 +216,8 @@
 
 
 def merge_kernel(
-    tiles, lookup_hbm, across_ref, high_ref, low_ref, x_ref, o_ref, lookup_ref, rows, sem
+    tiles, push_ref, across_ref, high_ref, low_ref, x_ref, o_ref, rows
 ):
-    @pl.when(pl.program_id(0) == 0)
-    def _():
-        lookup = pltpu.make_async_copy(lookup_hbm, lookup_ref, sem)
-        lookup.start()
-        lookup.wait()
-
-    code = wide_code()
     across = across_ref[...]
     pairs = [(tile, s) for tile in range(tiles) for s in range(4)]
     size = 64 * len(pairs)
@@ -214,23 +236,12 @@
             for p in range(len(pairs)):
                 rows[64 * p : 64 * p + 64, lane : lane + 128] = high[:, 128 * p : 128 * p + 128]
                 rows[size + 64 * p : size + 64 * p + 64, lane : lane + 128] = low[:, 128 * p : 128 * p + 128]
-    table = [
-        tables(node_at(iota(0)), node_at(iota(1) // 16), narrow_place() * 8 + code % 2 * 4 + s, 0.0, 0.0, 4.0)
-        for s in range(4)
-    ]
-    units = []
-    for tile, s in pairs:
-        box = lookup_ref[8, (pl.program_id(0) * tiles + tile) * 8 + code // 2].astype(jnp.int32)
-        center_a = (box // 8).astype(jnp.float32) / 8.0 + 0.0625
-        center_d = (box % 8).astype(jnp.float32) / 8.0 + 0.0625
-        speed = lookup_ref[box // 8, box % 8]
-        units.append(unit(center_a * table[s][0] + (center_d * table[s][1] + speed * table[s][2])))
     for t0 in range(2):
         wh, wl = high_ref[:, 256 * t0 : 256 * t0 + 256], low_ref[:, 256 * t0 : 256 * t0 + 256]
         both = jnp.dot(rows[...], wh, preferred_element_type=jnp.float32)
         total = both[:size] + both[size:] + jnp.dot(rows[:size], wl, preferred_element_type=jnp.float32)
         for p, (tile, s) in enumerate(pairs):
-            cosine, sine = units[p]
+            cosine, sine = push_ref[tile, s, 0], push_ref[tile, s, 1]
             for t3 in range(2):
                 for t1 in range(2):
                     at = 64 * p + 16 * t3 + 8 * t1
@@ -257,16 +268,21 @@
 def pull(lookup, x):
     return pl.pallas_call(
         pull_kernel,
-        out_shape=jax.ShapeDtypeStruct((8, 8, 8, 2, 8, 128), jnp.float32),
+        out_shape=(
+            jax.ShapeDtypeStruct((8, 8, 8, 2, 8, 128), jnp.float32),
+            jax.ShapeDtypeStruct((8, 4, 2, 8, 128), jnp.float32),
+        ),
         in_specs=[ANY, ANY],
-        out_specs=ANY,
+        out_specs=(ANY, ANY),
         scratch_shapes=[
             LOOKUP,
             pltpu.SMEM((64,), jnp.int32),
             pltpu.VMEM((128, 2048), jnp.bfloat16),
             pltpu.VMEM((8, 64, 2, 8, 128), jnp.float32),
             pltpu.VMEM((8, 8, 8, 2, 8, 128), jnp.float32),
+            pltpu.VMEM((8, 4, 2, 8, 128), jnp.float32),
             pltpu.VMEM((512, 2048), jnp.float32),
+            pltpu.SemaphoreType.DMA,
             pltpu.SemaphoreType.DMA,
             pltpu.SemaphoreType.DMA((8,)),
             pltpu.SemaphoreType.DMA((8,)),
@@ -275,31 +291,31 @@
     )(lookup, x)
 
 
-def merge(lookup, x, tiles=2):
+def merge(push, x, tiles=4):
     high, low = down_matrix()
     return pl.pallas_call(
         lambda *refs: merge_kernel(tiles, *refs),
         grid=(8 // tiles,),
         out_shape=jax.ShapeDtypeStruct((8, 8, 2, 4, 2, 8, 128), jnp.float32),
         in_specs=[
-            ANY,
+            pl.BlockSpec((tiles, 4, 2, 8, 128), lambda i: (i, 0, 0, 0, 0)),
             whole((64, 192)),
             whole((512, 512)),
             whole((512, 512)),
             pl.BlockSpec((16, 4, tiles, 2, 8, 128), lambda i: (0, 0, i, 0, 0, 0)),
         ],
         out_specs=pl.BlockSpec((8, tiles, 2, 4, 2, 8, 128), lambda i: (0, i, 0, 0, 0, 0, 0)),
-        scratch_shapes=[LOOKUP, pltpu.VMEM((512 * tiles, 512), jnp.bfloat16), pltpu.SemaphoreType.DMA],
-        compiler_params=pltpu.CompilerParams(vmem_limit_bytes=32 * 2**20),
-    )(lookup, across_matrix(), high, low, x)
+        scratch_shapes=[pltpu.VMEM((512 * tiles, 512), jnp.bfloat16)],
+        compiler_params=pltpu.CompilerParams(vmem_limit_bytes=40 * 2**20),
+    )(push, across_matrix(), high, low, x)
 
 
 def local(weights_in, medium_speed, target_order):
     speeds = jnp.pad(medium_speed, ((0, 0), (0, 56)))
     lookup = jnp.concatenate([speeds, target_order.astype(jnp.float32)[None]], axis=0)
-    turned = pull(lookup, weights_in[0])
+    turned, push = pull(lookup, weights_in[0])
     gathered = lax.all_to_all(turned.reshape(16, 4, 8, 2, 8, 128), WIDE, 0, 0, tiled=True)
-    merged = merge(lookup, gathered)
+    merged = merge(push, gathered)
     chunks = merged.reshape(128, 4, 2, 8, 128)
     spread = lax.all_to_all(chunks, ("z_hi", "y", "z_lo", "x", "core"), 0, 0, tiled=True)
     return spread.reshape(1, 8, 64, 2, 8, 128)

time: 132 us -> 131 us (level)
  no operation moved by 1% of the time
where the time goes in v6:
time: 131 us
  blocking collectives  118 us (90%)
  Pallas kernels  9.14 us (7%)
  local copies, waits for them, and re-layouts  2.03 us (2%)
  other arithmetic  1.35 us (1%)
    all_to_all x1, blocking collectives, local(): lax.all_to_all(turned.reshape(16, 4, 8, 2, 8, 128), WIDE, 0, 0, tiled=True)  59.9 us
    all_to_all x1, blocking collectives, local(): lax.all_to_all(chunks, ('z_hi', 'y', 'z_lo', 'x', 'core'), 0, 0, tiled=True)  58.1 us
    pallas_call x1, Pallas kernels, merge(): pl.pallas_call(lambda *refs: merge_kernel(tiles, *refs), grid=(8 // tiles...  5.64 us
    pallas_call x1, Pallas kernels, pull(): pl.pallas_call(pull_kernel, out_shape=(jax.ShapeDtypeStruct((8, 8, 8, 2,...  3.5 us

profile of v6, /device:TPU:1, one launch (start us, length us, event | category | flops | bytes accessed | tf_op | source)
XLA Modules:
  0.0 130.6 jit_solution(2070677901143357672)
XLA Ops:
  0.0 0.7 convert_bitcast_fusion
  0.7 0.7 select_maximum_fusion.lookup_hbm
  1.4 3.5 %shard_map.64 = (f32[8,8,8,2,8,128]{5,4,3,2,1,0:T(8,128)S(1)}, f32[8,4,2,8,128]{4,3,2,1,0:T(8,128)S(1)}) custom-call(f32[9,64]{1,0:T(8,128)S(1)} %select_maximum_fusion.lookup_hbm, f32[8,64,2,8,128]{4,3,2,1,0:T(8,128)} %bitcast.9), custom_call_target="tpu_custom_call" | custom-call | tf_op jit(solution)/shard_map/pallas_call | solution.py:269
  4.9 0.0 copy-start
  4.9 0.0 copy-start.1
  4.9 0.0 copy-start.2
  4.9 59.9 %all_to_all.10.refs_4_ = f32[16,4,8,2,8,128]{5,4,3,2,1,0:T(8,128)S(1)} all-to-all(f32[16,4,8,2,8,128]{5,4,3,2,1,0:T(8,128)S(1)} %bitcast.7), channel_id=1, replica_groups=mesh['z_hi'=2,'y'=4,'core'=2,'z_lo'=2,'x'=4] {'z_hi','y','core'}, dimensions={0} | all-to-all | bytes 8388608 | tf_op jit(solution)/shard_map/all_to_all | solution.py:317
  64.8 0.0 copy-done
  64.8 0.0 copy-done.1
  64.8 0.0 copy-done.2
  64.8 5.6 %shard_map.65 = f32[8,8,2,4,2,8,128]{6,5,4,3,2,1,0:T(8,128)S(1)} custom-call(f32[8,4,2,8,128]{4,3,2,1,0:T(8,128)S(1)} %get-tuple-element.7.refs_0_, bf16[64,192]{1,0:T(8,128)(2,1)S(1)} %copy-done.2, bf16[512,512]{1,0:T(8,128)(2,1)S(1)} %copy-done.1, bf16[512,512]{1,0:T(8,128)(2,1)S(1)} %copy-done, f32[16,4,8,2,8,128]{5,4,3,2,1,0:T(8,128)S(1)} %all_to_all.10.refs_4_), custom_call_target="tpu_custom_call" | custom-call | tf_op jit(solution)/shard_map/pallas_call | solution.py:296
  70.5 58.1 %all_to_all.11 = f32[128,4,2,8,128]{4,3,2,1,0:T(8,128)S(1)} all-to-all(f32[128,4,2,8,128]{4,3,2,1,0:T(8,128)S(1)} %bitcast.6), channel_id=1, replica_groups=mesh['z_hi'=2,'y'=4,'core'=2,'z_lo'=2,'x'=4] {'z_hi','y','z_lo','x','core'}, dimensions={0} | all-to-all | bytes 8388608 | tf_op jit(solution)/shard_map/all_to_all | solution.py:320
  128.6 2.0 %copy.8 = f32[1,8,64,2,8,128]{5,4,3,2,1,0:T(8,128)} copy(f32[1,8,64,2,8,128]{5,4,3,2,1,0:T(8,128)S(1)} %bitcast.8) | data formatting | bytes 8388608
Async XLA Ops:
  4.9 60.0 %copy-start = (bf16[512,512]{1,0:T(8,128)(2,1)S(1)}, bf16[512,512]{1,0:T(8,128)(2,1)}, u32[]{:S(2)}) copy-start(bf16[512,512]{1,0:T(8,128)(2,1)} %constant.11.clone.refs_3_) | copy-start | bytes 1572868
  4.9 60.0 %copy-start.1 = (bf16[512,512]{1,0:T(8,128)(2,1)S(1)}, bf16[512,512]{1,0:T(8,128)(2,1)}, u32[]{:S(2)}) copy-start(bf16[512,512]{1,0:T(8,128)(2,1)} %constant.10.clone.refs_2_) | copy-start | bytes 1572868
  4.9 60.0 %copy-start.2 = (bf16[64,192]{1,0:T(8,128)(2,1)S(1)}, bf16[64,192]{1,0:T(8,128)(2,1)}, u32[]{:S(2)}) copy-start(bf16[64,192]{1,0:T(8,128)(2,1)} %constant.9.clone.refs_1_) | copy-start | bytes 73732

commit v7 on v6

--- a/solution.py
+++ b/solution.py
@@ -116,24 +116,25 @@
 
 
 def pull_kernel(
-    lookup_hbm,
+    order_hbm,
+    speed_hbm,
     x_hbm,
-    o_hbm,
-    push_hbm,
-    lookup_ref,
+    o_ref,
+    push_ref,
+    order_ref,
+    speed_ref,
     place_ref,
     spread_ref,
     x_ref,
-    o_ref,
-    push_ref,
     turned,
-    sem,
-    push_sem,
+    order_sem,
+    speed_sem,
     in_sems,
-    out_sems,
 ):
-    lookup = pltpu.make_async_copy(lookup_hbm, lookup_ref, sem)
-    lookup.start()
+    order_copy = pltpu.make_async_copy(order_hbm, order_ref, order_sem)
+    speed_copy = pltpu.make_async_copy(speed_hbm, speed_ref, speed_sem)
+    order_copy.start()
+    speed_copy.start()
     arrivals = [pltpu.make_async_copy(x_hbm.at[s], x_ref.at[s], in_sems.at[s]) for s in range(8)]
     for arrival in arrivals:
         arrival.start()
@@ -155,15 +156,16 @@
     for box in range(16):
         same = jnp.where(row == box % 2 * 8 + point, 1.0, 0.0).astype(jnp.bfloat16)
         spread_ref[box // 2 * 16 : box // 2 * 16 + 16, 128 * box : 128 * box + 128] = same
-    lookup.wait()
+    order_copy.wait()
+    speed_copy.wait()
     speed = []
     for high in range(4):
         value = jnp.zeros((8, 128), jnp.float32)
         for low in range(16):
-            value = jnp.where(lane // 8 == low, lookup_ref[2 * high + low // 8, low % 8], value)
+            value = jnp.where(lane // 8 == low, speed_ref[2 * high + low // 8, low % 8], value)
         speed.append(value)
     for j in range(64):
-        place_ref[lookup_ref[8, j].astype(jnp.int32)] = j % 8 * 8 + j // 8
+        place_ref[order_ref[j]] = j % 8 * 64 + j // 8
 
     def spread(group):
         both_supers = (2 * group, 2 * group + 1)
@@ -178,36 +180,27 @@
         tables(node_a, node_at(lane // 16), narrow_place() * 8 + code % 2 * 4 + s, 0.0, 0.0, 4.0) for s in range(4)
     ]
     for tile in range(8):
-        box = lookup_ref[8, tile * 8 + code // 2].astype(jnp.int32)
+        box = order_ref[tile * 8 + code // 2]
         across = (box // 8).astype(jnp.float32) / 8.0 + 0.0625
         down = (box % 8).astype(jnp.float32) / 8.0 + 0.0625
-        at_box = lookup_ref[box // 8, box % 8]
+        at_box = speed_ref[box // 8, box % 8]
         for s in range(4):
             cosine, sine = unit(across * table[s][0] + (down * table[s][1] + at_box * table[s][2]))
             push_ref[tile, s, 0] = cosine
             push_ref[tile, s, 1] = sine
-    push_copy = pltpu.make_async_copy(push_ref, push_hbm, push_sem)
-    push_copy.start()
-    departures = []
     flat = o_ref.reshape(512, 2, 8, 128)
     for s in range(8):
         arrivals[s].wait()
         if s % 2 == 1 and s < 7:
             spread(s // 2 + 1)
         for box in range(64):
-            place = place_ref[box] + 64 * s
+            place = place_ref[box] + 8 * s
             at, lanes = 64 * s + 8 * (box // 16), 128 * (box % 16)
             cosine = turned[at : at + 8, lanes : lanes + 128]
             sine = turned[32 + at : 40 + at, lanes : lanes + 128]
             real, imag = x_ref[s, box, 0], x_ref[s, box, 1]
             flat[place, 0] = real * cosine + imag * sine
             flat[place, 1] = imag * cosine - real * sine
-        departure = pltpu.make_async_copy(o_ref.at[s], o_hbm.at[:, s], out_sems.at[s])
-        departure.start()
-        departures.append(departure)
-    push_copy.wait()
-    for departure in departures:
-        departure.wait()
 
 
 def split(value):
@@ -219,7 +212,12 @@
     tiles, push_ref, across_ref, high_ref, low_ref, x_ref, o_ref, rows
 ):
     across = across_ref[...]
-    pairs = [(tile, s) for tile in range(tiles) for s in range(4)]
+    for first in range(0, 8, tiles):
+        merge_tiles(range(first, first + tiles), push_ref, across, high_ref, low_ref, x_ref, o_ref, rows)
+
+
+def merge_tiles(steps, push_ref, across, high_ref, low_ref, x_ref, o_ref, rows):
+    pairs = [(tile, s) for tile in steps for s in range(4)]
     size = 64 * len(pairs)
     for g2 in range(2):
         for g0 in range(2):
@@ -258,62 +256,47 @@
 
 
 ANY = pl.BlockSpec(memory_space=pl.ANY)
-LOOKUP = pltpu.SMEM((9, 64), jnp.float32)
-
-
-def whole(shape):
-    return pl.BlockSpec(shape, lambda i: (0,) * len(shape))
-
-
-def pull(lookup, x):
+VMEM = pl.BlockSpec(memory_space=pltpu.VMEM)
+
+
+def pull(order, speed, x):
     return pl.pallas_call(
         pull_kernel,
         out_shape=(
             jax.ShapeDtypeStruct((8, 8, 8, 2, 8, 128), jnp.float32),
             jax.ShapeDtypeStruct((8, 4, 2, 8, 128), jnp.float32),
         ),
-        in_specs=[ANY, ANY],
-        out_specs=(ANY, ANY),
+        in_specs=[ANY, ANY, ANY],
+        out_specs=(VMEM, VMEM),
         scratch_shapes=[
-            LOOKUP,
+            pltpu.SMEM((64,), jnp.int32),
+            pltpu.SMEM((8, 8), jnp.float32),
             pltpu.SMEM((64,), jnp.int32),
             pltpu.VMEM((128, 2048), jnp.bfloat16),
             pltpu.VMEM((8, 64, 2, 8, 128), jnp.float32),
-            pltpu.VMEM((8, 8, 8, 2, 8, 128), jnp.float32),
-            pltpu.VMEM((8, 4, 2, 8, 128), jnp.float32),
             pltpu.VMEM((512, 2048), jnp.float32),
             pltpu.SemaphoreType.DMA,
             pltpu.SemaphoreType.DMA,
             pltpu.SemaphoreType.DMA((8,)),
-            pltpu.SemaphoreType.DMA((8,)),
         ],
         compiler_params=pltpu.CompilerParams(vmem_limit_bytes=48 * 2**20),
-    )(lookup, x)
-
-
-def merge(push, x, tiles=4):
+    )(order, speed, x)
+
+
+def merge(push, x, tiles=2):
     high, low = down_matrix()
     return pl.pallas_call(
         lambda *refs: merge_kernel(tiles, *refs),
-        grid=(8 // tiles,),
         out_shape=jax.ShapeDtypeStruct((8, 8, 2, 4, 2, 8, 128), jnp.float32),
-        in_specs=[
-            pl.BlockSpec((tiles, 4, 2, 8, 128), lambda i: (i, 0, 0, 0, 0)),
-            whole((64, 192)),
-            whole((512, 512)),
-            whole((512, 512)),
-            pl.BlockSpec((16, 4, tiles, 2, 8, 128), lambda i: (0, 0, i, 0, 0, 0)),
-        ],
-        out_specs=pl.BlockSpec((8, tiles, 2, 4, 2, 8, 128), lambda i: (0, i, 0, 0, 0, 0, 0)),
+        in_specs=[VMEM] * 5,
+        out_specs=VMEM,
         scratch_shapes=[pltpu.VMEM((512 * tiles, 512), jnp.bfloat16)],
         compiler_params=pltpu.CompilerParams(vmem_limit_bytes=40 * 2**20),
     )(push, across_matrix(), high, low, x)
 
 
 def local(weights_in, medium_speed, target_order):
-    speeds = jnp.pad(medium_speed, ((0, 0), (0, 56)))
-    lookup = jnp.concatenate([speeds, target_order.astype(jnp.float32)[None]], axis=0)
-    turned, push = pull(lookup, weights_in[0])
+    turned, push = pull(target_order, medium_speed, weights_in[0])
     gathered = lax.all_to_all(turned.reshape(16, 4, 8, 2, 8, 128), WIDE, 0, 0, tiled=True)
     merged = merge(push, gathered)
     chunks = merged.reshape(128, 4, 2, 8, 128)

time: 131 us -> 130 us (level)
  other arithmetic: 1.35 us -> 0 us
  local copies, waits for them, and re-layouts: 2.03 us -> 3.37 us
    unnamed x7 -> x11, local copies, waits for them, and re-layouts: 2.03 us -> 3.37 us
where the time goes in v7:
time: 130 us
  blocking collectives  118 us (91%)
  Pallas kernels  8.03 us (6%)
  local copies, waits for them, and re-layouts  3.37 us (3%)
    all_to_all x1, blocking collectives, local(): lax.all_to_all(turned.reshape(16, 4, 8, 2, 8, 128), WIDE, 0, 0, tiled=True)  59.9 us
    all_to_all x1, blocking collectives, local(): lax.all_to_all(chunks, ('z_hi', 'y', 'z_lo', 'x', 'core'), 0, 0, tiled=True)  58.1 us
    pallas_call x1, Pallas kernels, merge(): pl.pallas_call(lambda *refs: merge_kernel(tiles, *refs), out_shape=jax.Sh...  5.02 us
    unnamed x11, local copies, waits for them, and re-layouts  3.37 us
    pallas_call x1, Pallas kernels, pull(): pl.pallas_call(pull_kernel, out_shape=(jax.ShapeDtypeStruct((8, 8, 8, 2,...  3.01 us

profile of v7, /device:TPU:1, one launch (start us, length us, event | category | flops | bytes accessed | tf_op | source)
XLA Modules:
  0.0 129.5 jit_solution(5047719978672980568)
XLA Ops:
  0.0 0.0 copy-start.3
  0.0 0.7 copy-done.3
  0.7 0.0 copy-start.4
  0.7 0.7 copy-done.4
  1.3 3.0 %shard_map.64 = (f32[8,8,8,2,8,128]{5,4,3,2,1,0:T(8,128)S(1)}, f32[8,4,2,8,128]{4,3,2,1,0:T(8,128)S(1)}) custom-call(s32[64]{0:T(128)S(1)} %copy-done.4, f32[8,8]{1,0:T(8,128)S(1)} %copy-done.3, f32[8,64,2,8,128]{4,3,2,1,0:T(8,128)} %bitcast.7), custom_call_target="tpu_custom_call" | custom-call | tf_op jit(solution)/shard_map/pallas_call | solution.py:263
  4.4 0.0 copy-start
  4.4 0.0 copy-start.1
  4.4 0.0 copy-start.2
  4.4 59.9 %all_to_all.10.refs_4_ = f32[16,4,8,2,8,128]{5,4,3,2,1,0:T(8,128)S(1)} all-to-all(f32[16,4,8,2,8,128]{5,4,3,2,1,0:T(8,128)S(1)} %bitcast.5), channel_id=1, replica_groups=mesh['z_hi'=2,'y'=4,'core'=2,'z_lo'=2,'x'=4] {'z_hi','y','core'}, dimensions={0} | all-to-all | bytes 8388608 | tf_op jit(solution)/shard_map/all_to_all | solution.py:300
  64.3 0.0 copy-done
  64.3 0.0 copy-done.1
  64.3 0.0 copy-done.2
  64.3 5.0 %shard_map.65 = f32[8,8,2,4,2,8,128]{6,5,4,3,2,1,0:T(8,128)S(1)} custom-call(f32[8,4,2,8,128]{4,3,2,1,0:T(8,128)S(1)} %get-tuple-element.7.refs_0_, bf16[64,192]{1,0:T(8,128)(2,1)S(1)} %copy-done.2, bf16[512,512]{1,0:T(8,128)(2,1)S(1)} %copy-done.1, bf16[512,512]{1,0:T(8,128)(2,1)S(1)} %copy-done, f32[16,4,8,2,8,128]{5,4,3,2,1,0:T(8,128)S(1)} %all_to_all.10.refs_4_), custom_call_target="tpu_custom_call" | custom-call | tf_op jit(solution)/shard_map/pallas_call | solution.py:288
  69.4 58.1 %all_to_all.11 = f32[128,4,2,8,128]{4,3,2,1,0:T(8,128)S(1)} all-to-all(f32[128,4,2,8,128]{4,3,2,1,0:T(8,128)S(1)} %bitcast.4), channel_id=1, replica_groups=mesh['z_hi'=2,'y'=4,'core'=2,'z_lo'=2,'x'=4] {'z_hi','y','z_lo','x','core'}, dimensions={0} | all-to-all | bytes 8388608 | tf_op jit(solution)/shard_map/all_to_all | solution.py:303
  127.5 2.0 %copy.8 = f32[1,8,64,2,8,128]{5,4,3,2,1,0:T(8,128)} copy(f32[1,8,64,2,8,128]{5,4,3,2,1,0:T(8,128)S(1)} %bitcast.6) | data formatting | bytes 8388608
Async XLA Ops:
  0.0 0.7 copy-start.3
  0.7 0.7 copy-start.4
  4.4 60.0 %copy-start = (bf16[512,512]{1,0:T(8,128)(2,1)S(1)}, bf16[512,512]{1,0:T(8,128)(2,1)}, u32[]{:S(2)}) copy-start(bf16[512,512]{1,0:T(8,128)(2,1)} %constant.8.clone.refs_3_) | copy-start | bytes 1572868
  4.4 60.0 %copy-start.1 = (bf16[512,512]{1,0:T(8,128)(2,1)S(1)}, bf16[512,512]{1,0:T(8,128)(2,1)}, u32[]{:S(2)}) copy-start(bf16[512,512]{1,0:T(8,128)(2,1)} %constant.7.clone.refs_2_) | copy-start | bytes 1572868
  4.4 60.0 %copy-start.2 = (bf16[64,192]{1,0:T(8,128)(2,1)S(1)}, bf16[64,192]{1,0:T(8,128)(2,1)}, u32[]{:S(2)}) copy-start(bf16[64,192]{1,0:T(8,128)(2,1)} %constant.6.clone.refs_1_) | copy-start | bytes 73732

commit v8 on v7

--- a/solution.py
+++ b/solution.py
@@ -179,20 +179,20 @@
     table = [
         tables(node_a, node_at(lane // 16), narrow_place() * 8 + code % 2 * 4 + s, 0.0, 0.0, 4.0) for s in range(4)
     ]
-    for tile in range(8):
-        box = order_ref[tile * 8 + code // 2]
-        across = (box // 8).astype(jnp.float32) / 8.0 + 0.0625
-        down = (box % 8).astype(jnp.float32) / 8.0 + 0.0625
-        at_box = speed_ref[box // 8, box % 8]
-        for s in range(4):
-            cosine, sine = unit(across * table[s][0] + (down * table[s][1] + at_box * table[s][2]))
-            push_ref[tile, s, 0] = cosine
-            push_ref[tile, s, 1] = sine
     flat = o_ref.reshape(512, 2, 8, 128)
     for s in range(8):
         arrivals[s].wait()
         if s % 2 == 1 and s < 7:
             spread(s // 2 + 1)
+        at_tile = order_ref[s * 8 + code // 2]
+        across = (at_tile // 8).astype(jnp.float32) / 8.0 + 0.0625
+        down = (at_tile % 8).astype(jnp.float32) / 8.0 + 0.0625
+        at_box = speed_ref[at_tile // 8, at_tile % 8]
+        turns = [across * part[0] + (down * part[1] + at_box * part[2]) for part in table]
+        cosine, sine = unit(jnp.concatenate(turns, axis=0))
+        for k in range(4):
+            push_ref[s, k, 0] = cosine[8 * k : 8 * k + 8]
+            push_ref[s, k, 1] = sine[8 * k : 8 * k + 8]
         for box in range(64):
             place = place_ref[box] + 8 * s
             at, lanes = 64 * s + 8 * (box // 16), 128 * (box % 16)

time: 130 us -> 130 us (level)
  no operation moved by 1% of the time
where the time goes in v8:
time: 130 us
  blocking collectives  118 us (91%)
  Pallas kernels  8.13 us (6%)
  local copies, waits for them, and re-layouts  3.37 us (3%)
    all_to_all x1, blocking collectives, local(): lax.all_to_all(turned.reshape(16, 4, 8, 2, 8, 128), WIDE, 0, 0, tiled=True)  59.9 us
    all_to_all x1, blocking collectives, local(): lax.all_to_all(chunks, ('z_hi', 'y', 'z_lo', 'x', 'core'), 0, 0, tiled=True)  58.1 us
    pallas_call x1, Pallas kernels, merge(): pl.pallas_call(lambda *refs: merge_kernel(tiles, *refs), out_shape=jax.Sh...  5.03 us
    unnamed x11, local copies, waits for them, and re-layouts  3.37 us
    pallas_call x1, Pallas kernels, pull(): pl.pallas_call(pull_kernel, out_shape=(jax.ShapeDtypeStruct((8, 8, 8, 2,...  3.1 us

profile of v8, /device:TPU:1, one launch (start us, length us, event | category | flops | bytes accessed | tf_op | source)
XLA Modules:
  0.0 129.6 jit_solution(12270260145191653766)
XLA Ops:
  0.0 0.0 copy-start.3
  0.0 0.7 copy-done.3
  0.7 0.0 copy-start.4
  0.7 0.7 copy-done.4
  1.3 3.1 %shard_map.64 = (f32[8,8,8,2,8,128]{5,4,3,2,1,0:T(8,128)S(1)}, f32[8,4,2,8,128]{4,3,2,1,0:T(8,128)S(1)}) custom-call(s32[64]{0:T(128)S(1)} %copy-done.4, f32[8,8]{1,0:T(8,128)S(1)} %copy-done.3, f32[8,64,2,8,128]{4,3,2,1,0:T(8,128)} %bitcast.7), custom_call_target="tpu_custom_call" | custom-call | tf_op jit(solution)/shard_map/pallas_call | solution.py:263
  4.5 0.0 copy-start
  4.5 0.0 copy-start.1
  4.5 0.0 copy-start.2
  4.5 59.9 %all_to_all.10.refs_4_ = f32[16,4,8,2,8,128]{5,4,3,2,1,0:T(8,128)S(1)} all-to-all(f32[16,4,8,2,8,128]{5,4,3,2,1,0:T(8,128)S(1)} %bitcast.5), channel_id=1, replica_groups=mesh['z_hi'=2,'y'=4,'core'=2,'z_lo'=2,'x'=4] {'z_hi','y','core'}, dimensions={0} | all-to-all | bytes 8388608 | tf_op jit(solution)/shard_map/all_to_all | solution.py:300
  64.4 0.0 copy-done
  64.4 0.0 copy-done.1
  64.4 0.0 copy-done.2
  64.4 5.0 %shard_map.65 = f32[8,8,2,4,2,8,128]{6,5,4,3,2,1,0:T(8,128)S(1)} custom-call(f32[8,4,2,8,128]{4,3,2,1,0:T(8,128)S(1)} %get-tuple-element.7.refs_0_, bf16[64,192]{1,0:T(8,128)(2,1)S(1)} %copy-done.2, bf16[512,512]{1,0:T(8,128)(2,1)S(1)} %copy-done.1, bf16[512,512]{1,0:T(8,128)(2,1)S(1)} %copy-done, f32[16,4,8,2,8,128]{5,4,3,2,1,0:T(8,128)S(1)} %all_to_all.10.refs_4_), custom_call_target="tpu_custom_call" | custom-call | tf_op jit(solution)/shard_map/pallas_call | solution.py:288
  69.5 58.1 %all_to_all.11 = f32[128,4,2,8,128]{4,3,2,1,0:T(8,128)S(1)} all-to-all(f32[128,4,2,8,128]{4,3,2,1,0:T(8,128)S(1)} %bitcast.4), channel_id=1, replica_groups=mesh['z_hi'=2,'y'=4,'core'=2,'z_lo'=2,'x'=4] {'z_hi','y','z_lo','x','core'}, dimensions={0} | all-to-all | bytes 8388608 | tf_op jit(solution)/shard_map/all_to_all | solution.py:303
  127.6 2.0 %copy.8 = f32[1,8,64,2,8,128]{5,4,3,2,1,0:T(8,128)} copy(f32[1,8,64,2,8,128]{5,4,3,2,1,0:T(8,128)S(1)} %bitcast.6) | data formatting | bytes 8388608
Async XLA Ops:
  0.0 0.7 copy-start.3
  0.7 0.7 copy-start.4
  4.5 60.0 %copy-start = (bf16[512,512]{1,0:T(8,128)(2,1)S(1)}, bf16[512,512]{1,0:T(8,128)(2,1)}, u32[]{:S(2)}) copy-start(bf16[512,512]{1,0:T(8,128)(2,1)} %constant.8.clone.refs_3_) | copy-start | bytes 1572868
  4.5 60.0 %copy-start.1 = (bf16[512,512]{1,0:T(8,128)(2,1)S(1)}, bf16[512,512]{1,0:T(8,128)(2,1)}, u32[]{:S(2)}) copy-start(bf16[512,512]{1,0:T(8,128)(2,1)} %constant.7.clone.refs_2_) | copy-start | bytes 1572868
  4.5 60.0 %copy-start.2 = (bf16[64,192]{1,0:T(8,128)(2,1)S(1)}, bf16[64,192]{1,0:T(8,128)(2,1)}, u32[]{:S(2)}) copy-start(bf16[64,192]{1,0:T(8,128)(2,1)} %constant.6.clone.refs_1_) | copy-start | bytes 73732

commit v9 on v7

--- a/solution.py
+++ b/solution.py
@@ -189,18 +189,20 @@
             push_ref[tile, s, 0] = cosine
             push_ref[tile, s, 1] = sine
     flat = o_ref.reshape(512, 2, 8, 128)
-    for s in range(8):
-        arrivals[s].wait()
-        if s % 2 == 1 and s < 7:
-            spread(s // 2 + 1)
+    for group in range(4):
+        for s in (2 * group, 2 * group + 1):
+            arrivals[s].wait()
+        if group < 3:
+            spread(group + 1)
         for box in range(64):
-            place = place_ref[box] + 8 * s
-            at, lanes = 64 * s + 8 * (box // 16), 128 * (box % 16)
-            cosine = turned[at : at + 8, lanes : lanes + 128]
-            sine = turned[32 + at : 40 + at, lanes : lanes + 128]
-            real, imag = x_ref[s, box, 0], x_ref[s, box, 1]
-            flat[place, 0] = real * cosine + imag * sine
-            flat[place, 1] = imag * cosine - real * sine
+            place = place_ref[box]
+            for s in (2 * group, 2 * group + 1):
+                at, lanes = 64 * s + 8 * (box // 16), 128 * (box % 16)
+                cosine = turned[at : at + 8, lanes : lanes + 128]
+                sine = turned[32 + at : 40 + at, lanes : lanes + 128]
+                real, imag = x_ref[s, box, 0], x_ref[s, box, 1]
+                flat[place + 8 * s, 0] = real * cosine + imag * sine
+                flat[place + 8 * s, 1] = imag * cosine - real * sine
 
 
 def split(value):

time: 130 us -> 130 us (level)
  no operation moved by 1% of the time
where the time goes in v9:
time: 130 us
  blocking collectives  118 us (91%)
  Pallas kernels  8.02 us (6%)
  local copies, waits for them, and re-layouts  3.37 us (3%)
    all_to_all x1, blocking collectives, local(): lax.all_to_all(turned.reshape(16, 4, 8, 2, 8, 128), WIDE, 0, 0, tiled=True)  59.9 us
    all_to_all x1, blocking collectives, local(): lax.all_to_all(chunks, ('z_hi', 'y', 'z_lo', 'x', 'core'), 0, 0, tiled=True)  58.1 us
    pallas_call x1, Pallas kernels, merge(): pl.pallas_call(lambda *refs: merge_kernel(tiles, *refs), out_shape=jax.Sh...  5.02 us
    unnamed x11, local copies, waits for them, and re-layouts  3.37 us
    pallas_call x1, Pallas kernels, pull(): pl.pallas_call(pull_kernel, out_shape=(jax.ShapeDtypeStruct((8, 8, 8, 2,...  3 us

profile of v9, /device:TPU:1, one launch (start us, length us, event | category | flops | bytes accessed | tf_op | source)
XLA Modules:
  0.0 129.5 jit_solution(8018191358243830036)
XLA Ops:
  0.0 0.0 copy-start.3
  0.0 0.7 copy-done.3
  0.7 0.0 copy-start.4
  0.7 0.7 copy-done.4
  1.3 3.0 %shard_map.64 = (f32[8,8,8,2,8,128]{5,4,3,2,1,0:T(8,128)S(1)}, f32[8,4,2,8,128]{4,3,2,1,0:T(8,128)S(1)}) custom-call(s32[64]{0:T(128)S(1)} %copy-done.4, f32[8,8]{1,0:T(8,128)S(1)} %copy-done.3, f32[8,64,2,8,128]{4,3,2,1,0:T(8,128)} %bitcast.7), custom_call_target="tpu_custom_call" | custom-call | tf_op jit(solution)/shard_map/pallas_call | solution.py:265
  4.4 0.0 copy-start
  4.4 0.0 copy-start.1
  4.4 0.0 copy-start.2
  4.4 59.9 %all_to_all.10.refs_4_ = f32[16,4,8,2,8,128]{5,4,3,2,1,0:T(8,128)S(1)} all-to-all(f32[16,4,8,2,8,128]{5,4,3,2,1,0:T(8,128)S(1)} %bitcast.5), channel_id=1, replica_groups=mesh['z_hi'=2,'y'=4,'core'=2,'z_lo'=2,'x'=4] {'z_hi','y','core'}, dimensions={0} | all-to-all | bytes 8388608 | tf_op jit(solution)/shard_map/all_to_all | solution.py:302
  64.3 0.0 copy-done
  64.3 0.0 copy-done.1
  64.3 0.0 copy-done.2
  64.3 5.0 %shard_map.65 = f32[8,8,2,4,2,8,128]{6,5,4,3,2,1,0:T(8,128)S(1)} custom-call(f32[8,4,2,8,128]{4,3,2,1,0:T(8,128)S(1)} %get-tuple-element.7.refs_0_, bf16[64,192]{1,0:T(8,128)(2,1)S(1)} %copy-done.2, bf16[512,512]{1,0:T(8,128)(2,1)S(1)} %copy-done.1, bf16[512,512]{1,0:T(8,128)(2,1)S(1)} %copy-done, f32[16,4,8,2,8,128]{5,4,3,2,1,0:T(8,128)S(1)} %all_to_all.10.refs_4_), custom_call_target="tpu_custom_call" | custom-call | tf_op jit(solution)/shard_map/pallas_call | solution.py:290
  69.4 58.1 %all_to_all.11 = f32[128,4,2,8,128]{4,3,2,1,0:T(8,128)S(1)} all-to-all(f32[128,4,2,8,128]{4,3,2,1,0:T(8,128)S(1)} %bitcast.4), channel_id=1, replica_groups=mesh['z_hi'=2,'y'=4,'core'=2,'z_lo'=2,'x'=4] {'z_hi','y','z_lo','x','core'}, dimensions={0} | all-to-all | bytes 8388608 | tf_op jit(solution)/shard_map/all_to_all | solution.py:305
  127.5 2.0 %copy.8 = f32[1,8,64,2,8,128]{5,4,3,2,1,0:T(8,128)} copy(f32[1,8,64,2,8,128]{5,4,3,2,1,0:T(8,128)S(1)} %bitcast.6) | data formatting | bytes 8388608
Async XLA Ops:
  0.0 0.7 copy-start.3
  0.7 0.7 copy-start.4
  4.4 60.0 %copy-start = (bf16[512,512]{1,0:T(8,128)(2,1)S(1)}, bf16[512,512]{1,0:T(8,128)(2,1)}, u32[]{:S(2)}) copy-start(bf16[512,512]{1,0:T(8,128)(2,1)} %constant.8.clone.refs_3_) | copy-start | bytes 1572868
  4.4 60.0 %copy-start.1 = (bf16[512,512]{1,0:T(8,128)(2,1)S(1)}, bf16[512,512]{1,0:T(8,128)(2,1)}, u32[]{:S(2)}) copy-start(bf16[512,512]{1,0:T(8,128)(2,1)} %constant.7.clone.refs_2_) | copy-start | bytes 1572868
  4.4 60.0 %copy-start.2 = (bf16[64,192]{1,0:T(8,128)(2,1)S(1)}, bf16[64,192]{1,0:T(8,128)(2,1)}, u32[]{:S(2)}) copy-start(bf16[64,192]{1,0:T(8,128)(2,1)} %constant.6.clone.refs_1_) | copy-start | bytes 73732
